TPU v7x, 32 devices: a whole 2x2x4 slice. The times are simulated.
32 devices in a mesh: groups: 2 (over y), tiles: 4 (over z), heads: 2 (over x), cfg: 2 (over core).
Axes of the slice: x: 2, y: 2, z: 4, core: 2. Of those that a mesh axis runs over, the one named last changes fastest.
Arguments:
- latents: bfloat16 [6144, 3072], P(('groups', 'tiles'), ('heads', 'cfg')), parts along dimension 0, may hold values from -6 to 6
- modulation: float32 [6, 3072], P('groups'), parts along dimension 0, may hold values from -3 to 3
- qkv_weight: bfloat16 [3072, 1536], P(None, ('heads', 'cfg')), may hold values from -0.109375 to 0.109375
- query_gain: float32 [128], replicated, may hold values from 0.25 to 1.75
- key_gain: float32 [128], replicated, may hold values from 0.25 to 1.75
- text_kv: bfloat16 [512, 1024], P('groups', ('heads', 'cfg')), parts along dimension 0, may hold values from -72 to 72
- text_len: int32 [2], P('groups'), parts along dimension 0, may hold values from 128 to 256
- tile_ids: int32 [16], P(('groups', 'tiles')), parts along dimension 0, may hold values from 0 to 7, as said below
- windows: int32 [16, 27], P('groups'), parts along dimension 0, may hold values from 0 to 7, as said below
- proj_weight: bfloat16 [512, 3072], P(None, ('heads', 'cfg')), may hold values from -0.25 to 0.25
Outputs:
- updated: bfloat16 [6144, 3072], P(('groups', 'tiles'), ('heads', 'cfg')), parts along dimension 0
There are 2 independent parts, one for each index of `groups`. A program takes and returns all parts, laid end to end along the dimension named above; an argument that names none is the same for every part. Nothing has to cross between parts.
Inputs may be any that keep to these rules, and one draw needn't show every extreme that they name: Every entry of windows[t] names a tile at most one tile away from t along each dimension of the 2 x 2 x 2 tile grid, tile id (i * 2 + h) * 2 + w; entry 13 is t itself, and entries that name no other tile repeat t. `tile_ids`: slot s holds a tile id from (s // 2) * 2 to (s // 2) * 2 + 1; every id appears once.
All inputs are finite; a program needn't handle non-finite values.
Results may differ from a plain program's by a relative error of at most 0.0033.
The roundings to bfloat16 on the way count: a program that leaves them out, or rounds other values in their place, can miss the bound.
Values may be sent and summed in bfloat16 or wider, within the bound.
No kernel may reach another device: no remote copies, remote signals or barrier semaphores. Data moves between devices by JAX's collectives and lax.ppermute only.
A program may use at most 64 MiB of HBM per device.

v0:
```python
import functools
import math

import jax
import jax.numpy as jnp
from jax import lax
from jax.experimental import pallas as pl
from jax.experimental.pallas import tpu as pltpu
from jax.sharding import PartitionSpec as P

HD = 128
TILE = 384
TXT = 256
CHUNKS = ((0, 128), (128, 256), (384, 384))
LABEL_ROWS = 16

epsilon = 1e-06
LOG2E = math.log2(math.e)
FACTOR = LOG2E / math.sqrt(HD)

SMEM = pl.BlockSpec(memory_space=pltpu.SMEM)
VMEM = pl.BlockSpec(memory_space=pltpu.VMEM)
HBM = pl.BlockSpec(memory_space=pltpu.HBM)
ANY = pl.BlockSpec(memory_space=pl.ANY)
PROJECT_LIMIT = 24 * 2**20
ATTEND_LIMIT = 16 * 2**20
MERGE_LIMIT = 16 * 2**20
NT = (((1,), (1,)), ((), ()))


def rms_norm(values, gain):
    return values * lax.rsqrt(jnp.mean(values * values, axis=-1, keepdims=True) + epsilon) * gain


def project_kernel(count, after, starts, rows, place_ref, ids_ref, *refs):
    sources = refs[:count]
    refs = refs[:count] + refs[count + after :]
    modulation_ref, query_gain_ref, key_gain_ref, weight_ref = refs[count : count + 4]
    query_ref, kv_ref, pieces_ref, piece_sem = refs[count + 4 :]
    width = sources[0].shape[1]
    features = width * count
    spans = []
    piece_copies = []
    for place, (source, start) in enumerate(zip(sources, starts)):
        first = place_ref[place] * width
        if count > 1:
            first = pl.multiple_of(first, width)
        spans.append(pl.ds(first, width))
        piece_copies.append(
            pltpu.make_async_copy(source.at[start : start + rows, :], pieces_ref.at[place], piece_sem.at[place])
        )
    for copy in piece_copies:
        copy.start()
    total = 0.0
    for place, copy in enumerate(piece_copies):
        copy.wait()
        total = total + jnp.sum(pieces_ref[place].astype(jnp.float32), axis=1, keepdims=True)
    average = total / features
    spread = 0.0
    for place in range(count):
        centred = pieces_ref[place].astype(jnp.float32) - average
        spread = spread + jnp.sum(centred * centred, axis=1, keepdims=True)
    scale = lax.rsqrt(spread / features + epsilon)
    projected = 0.0
    for place, span in enumerate(spans):
        centred = pieces_ref[place].astype(jnp.float32) - average
        modulated = (
            centred * scale * (1.0 + modulation_ref[1:2, span]) + modulation_ref[0:1, span]
        ).astype(jnp.bfloat16)
        projected = projected + jnp.dot(modulated, weight_ref[span, :], preferred_element_type=jnp.float32)
    query_ref[...] = rms_norm(projected[:, :HD], query_gain_ref[...]).astype(jnp.bfloat16)
    kv_ref[:rows, :HD] = rms_norm(projected[:, HD : 2 * HD], key_gain_ref[...]).astype(jnp.bfloat16)
    kv_ref[:rows, HD:] = projected[:, 2 * HD :].astype(jnp.bfloat16)
    labels = kv_ref.shape[0] - rows
    if labels:
        lane = lax.broadcasted_iota(jnp.int32, (labels, 2 * HD), 1)
        label = jnp.full((labels, 2 * HD), ids_ref[0], jnp.int32)
        for slot in range(1, ids_ref.shape[0]):
            label = jnp.where(lane == slot, ids_ref[slot], label)
        kv_ref[rows:, :] = label.astype(jnp.float32).astype(jnp.bfloat16)


def preload_kernel(weight_ref, out_ref, sem):
    copy = pltpu.make_async_copy(weight_ref, out_ref, sem)
    copy.start()
    copy.wait()


def preload(weight):
    return pl.pallas_call(
        preload_kernel,
        out_shape=jax.ShapeDtypeStruct(weight.shape, weight.dtype),
        in_specs=[HBM],
        out_specs=VMEM,
        scratch_shapes=[pltpu.SemaphoreType.DMA],
        compiler_params=pltpu.CompilerParams(vmem_limit_bytes=ATTEND_LIMIT),
        cost_estimate=pl.CostEstimate(flops=0, bytes_accessed=4096, transcendentals=0),
    )(weight)


def project(places, ids, pieces, after, starts, modulation, weight, query_gain, key_gain, rows, labels):
    count = len(pieces)
    width = pieces[0].shape[1]
    return pl.pallas_call(
        functools.partial(project_kernel, count, len(after), starts, rows),
        out_shape=(
            jax.ShapeDtypeStruct((rows, HD), jnp.bfloat16),
            jax.ShapeDtypeStruct((rows + labels, 2 * HD), jnp.bfloat16),
        ),
        in_specs=[SMEM] * 2 + [HBM] * count + [ANY] * len(after) + [VMEM] * 4,
        out_specs=(VMEM, VMEM),
        scratch_shapes=[
            pltpu.VMEM((count, rows, width), jnp.bfloat16),
            pltpu.SemaphoreType.DMA((count,)),
        ],
        compiler_params=pltpu.CompilerParams(vmem_limit_bytes=PROJECT_LIMIT),
        cost_estimate=pl.CostEstimate(flops=rows, bytes_accessed=rows, transcendentals=rows),
    )(places, ids, *pieces, *after, modulation, query_gain, key_gain, weight)


def attend_block(query, shift, keys, values):
    scores = lax.dot_general(query, keys, NT, preferred_element_type=jnp.float32)
    strips = [
        jnp.exp2(scores[:, at : at + HD] * FACTOR - shift) for at in range(0, keys.shape[0], HD)
    ]
    weights = jnp.concatenate(strips, axis=1) if len(strips) > 1 else strips[0]
    product = jnp.dot(weights.astype(jnp.bfloat16), values, preferred_element_type=jnp.float32)
    return sum(strips), product


def segments(start, size):
    out = []
    at = start
    while at < start + size:
        end = min(start + size, (at // TILE + 1) * TILE)
        out.append((at - start, end - at, at // TILE))
        at = end
    return out


def attend_kernel(starts, plan, tiles, begin, held, last, stacked, ids_ref, own_ref, windows_ref, *refs):
    refs = list(refs)
    queries = [refs.pop(0) for _ in starts]
    kvs = [refs.pop(0) for _ in plan]
    if begin:
        length_ref, text_ref, query_gain_ref, key_gain_ref = [refs.pop(0) for _ in range(4)]
    if held:
        shift_in, total_in, accum_in = [refs.pop(0) for _ in range(3)]
    if last:
        out_ref = refs.pop(0)
    shift_ref, total_ref, accum_ref, query_ref = refs
    for start, piece in zip(starts, queries):
        query_ref[start : start + piece.shape[0], :] = piece[...]
    if begin:
        bound = (
            jnp.max(jnp.abs(query_gain_ref[...])) * jnp.max(jnp.abs(key_gain_ref[...])) * (1.02 * HD * FACTOR)
        )
        live = lax.broadcasted_iota(jnp.int32, (TILE, TXT), 1) < length_ref[0]
    for tile in sorted(begin + held):
        rows = slice(tile * TILE, (tile + 1) * TILE)
        if tile in begin:
            scores = lax.dot_general(query_ref[rows, :], text_ref[:, :HD], NT, preferred_element_type=jnp.float32)
            scores = jnp.where(live, scores * FACTOR, -jnp.inf)
            top = jnp.maximum(jnp.max(scores, axis=1, keepdims=True), bound)
            weights = jnp.exp2(scores - top)
            shift_ref[rows, :] = jnp.broadcast_to(top, (TILE, HD))
            total_ref[rows, :] = weights[:, :HD] + weights[:, HD:]
            accum_ref[rows, :] = jnp.dot(
                weights.astype(jnp.bfloat16), text_ref[:, HD:], preferred_element_type=jnp.float32
            )
        else:
            shift_ref[rows, :] = shift_in[rows, :]
            total_ref[rows, :] = total_in[rows, :]
            accum_ref[rows, :] = accum_in[rows, :]
        own = own_ref[tile]
        reach = 0
        for entry in range(windows_ref.shape[1]):
            reach = reach | (1 << windows_ref[own, entry])
        groups = {}
        for number, (source, start, size, wanted) in enumerate(plan):
            if tile in wanted:
                for at, length, slot in segments(start, size):
                    groups.setdefault((source, slot), []).append((number, slice(at, at + length)))
        for (source, slot), blocks in groups.items():

            def work(source, view, rows=rows, reach=reach, slot=slot, blocks=blocks):
                @pl.when(((reach >> ids_ref[source * tiles + slot]) & 1) > 0)
                def _():
                    parts = [
                        attend_block(
                            query_ref[rows, :], shift_ref[rows, :], view(number)[span, :HD], view(number)[span, HD:]
                        )
                        for number, span in blocks
                    ]
                    total_ref[rows, :] += sum(total for total, product in parts)
                    accum_ref[rows, :] += sum(product for total, product in parts)

            if stacked:

                def step(source, carry, work=work):
                    work(source, lambda number: kvs[number].at[source])
                    return carry

                lax.fori_loop(0, kvs[0].shape[0], step, 0)
            else:
                work(source, lambda number: kvs[number])
        if last:
            total = jnp.sum(total_ref[rows, :], axis=1, keepdims=True)
            out_ref[rows, :] = (accum_ref[rows, :] / total).astype(jnp.bfloat16)


def attend(tokens, queries, pieces, begin, held, start=(), state=(), last=False, stacked=False):
    ids, own_ids, windows = tokens
    tiles = own_ids.shape[0]
    rows = tiles * TILE
    part = jax.ShapeDtypeStruct((rows, HD), jnp.float32)
    scratch = [pltpu.VMEM((rows, HD), jnp.bfloat16)]
    if last:
        out_shape = jax.ShapeDtypeStruct((rows, HD), jnp.bfloat16)
        scratch = [pltpu.VMEM((rows, HD), jnp.float32)] * 3 + scratch
    else:
        out_shape = (part,) * 3
    keys = sum(piece[0].size // (2 * HD) for piece in pieces)
    extra = (tuple(start) if begin else ()) + tuple(state)
    return pl.pallas_call(
        functools.partial(
            attend_kernel, [at for at, array in queries], [piece[1:] for piece in pieces], tiles, begin, held, last, stacked
        ),
        out_shape=out_shape,
        in_specs=[SMEM] * 3
        + [VMEM] * (len(queries) + len(pieces))
        + ([SMEM] + [VMEM] * 3 if begin else [])
        + [VMEM] * len(state),
        out_specs=VMEM if last else (VMEM,) * 3,
        scratch_shapes=scratch,
        compiler_params=pltpu.CompilerParams(vmem_limit_bytes=ATTEND_LIMIT),
        cost_estimate=pl.CostEstimate(flops=rows * keys, bytes_accessed=rows * HD, transcendentals=rows),
    )(ids, own_ids, windows, *[array for at, array in queries], *[piece[0] for piece in pieces], *extra)


def merge_kernel(count, place_ref, *refs):
    pieces = refs[:count]
    weight_ref, latents_ref, gate_ref, out_ref, joined_ref = refs[count:]
    depth = pieces[0].shape[1]
    width = latents_ref.shape[1]
    if count > 1:
        gate = gate_ref[2:3, pl.ds(pl.multiple_of(place_ref[0] * width, width), width)]
        for place, piece in enumerate(pieces):
            joined_ref[:, pl.ds(pl.multiple_of(place_ref[place] * depth, depth), depth)] = piece[...]
        attended = joined_ref[...]
    else:
        gate = gate_ref[...]
        attended = pieces[0][...]
    product = jnp.dot(attended, weight_ref[...], preferred_element_type=jnp.float32)
    out_ref[...] = (latents_ref[...].astype(jnp.float32) + gate * product).astype(jnp.bfloat16)


def merge(places, pieces, weight, latents, gate):
    rows, width = latents.shape
    block = 256
    return pl.pallas_call(
        functools.partial(merge_kernel, len(pieces)),
        grid=(rows // block,),
        out_shape=jax.ShapeDtypeStruct((rows, width), jnp.bfloat16),
        in_specs=[SMEM]
        + [pl.BlockSpec((block, piece.shape[1]), lambda i: (i, 0)) for piece in pieces]
        + [
            pl.BlockSpec(weight.shape, lambda i: (0, 0)),
            pl.BlockSpec((block, width), lambda i: (i, 0)),
            pl.BlockSpec(gate.shape, lambda i: (0, 0)),
        ],
        out_specs=pl.BlockSpec((block, width), lambda i: (i, 0)),
        scratch_shapes=[pltpu.VMEM((block, len(pieces) * pieces[0].shape[1]), jnp.bfloat16)],
        compiler_params=pltpu.CompilerParams(vmem_limit_bytes=MERGE_LIMIT),
        cost_estimate=pl.CostEstimate(
            flops=2 * rows * width * weight.shape[0],
            bytes_accessed=rows * width * 4 + weight.size * 2 + rows * weight.shape[0] * 2,
            transcendentals=0,
        ),
    )(places, *pieces, weight, latents, gate)


def shifted(values, axis, size, by):
    return lax.ppermute(values, axis, [(at, (at + by) % size) for at in range(size)])


LINE = 4


NEAR = [(0, 1), (1, 0), (2, 3), (3, 2)]
AWAY = [(0, 2), (1, 3), (2, 0), (3, 1)]


def ordered(values, *before):
    return lax.optimization_barrier((values, *before))[0]


def body(
    heads_size,
    cfg_size,
    tiles_size,
    latents,
    modulation,
    qkv_weight,
    query_gain,
    key_gain,
    text_kv,
    text_len,
    tile_ids,
    windows,
    proj_weight,
):
    pairs = heads_size == 2 and cfg_size == 2
    stacked = tiles_size != LINE
    per_dev = tile_ids.shape[0]
    width = latents.shape[1]
    me = lax.axis_index(("heads", "cfg"))
    query_gain = query_gain[None, :]
    key_gain = key_gain[None, :]

    begin = (text_len, text_kv, query_gain, key_gain)
    everyone = list(range(per_dev))

    if pairs:
        parts = [latents[: CHUNKS[0][1]]]
        rest = ordered(latents, parts[0])
        parts += [rest[start : start + size] for start, size in CHUNKS[1:]]
        across = [shifted(part, "heads", 2, 1) for part in parts]
        beside = shifted(latents, "cfg", 2, 1)
        weight = preload(qkv_weight)
        places = jnp.stack([me, me ^ 1, me ^ 2, me ^ 3]).astype(jnp.int32)
    else:
        gathered = lax.all_gather(latents, ("heads", "cfg"), axis=1, tiled=True)
        weight = qkv_weight
        places = jnp.zeros((1,), jnp.int32)

    def project_chunk(number, before, after):
        start, size = CHUNKS[number]
        if pairs:
            far = ordered(across[number], *before)
            pieces = [latents, beside, far, shifted(far, "cfg", 2, 1)]
            starts = [start, start, 0, 0]
        else:
            pieces, starts = [gathered], [start]
        labels = 0 if number else LABEL_ROWS
        return project(
            places, tile_ids, pieces, after, starts, modulation, weight, query_gain, key_gain, size, labels
        )

    if stacked:
        made = [project_chunk(number, (), ()) for number in range(len(CHUNKS))]
        queries = [(start, query) for (start, size), (query, kv) in zip(CHUNKS, made)]
        spread = [lax.all_gather(kv, "tiles", axis=0) for query, kv in made]
        ids = spread[0][:, CHUNKS[0][1], :per_dev].reshape(-1).astype(jnp.int32)
        pieces = [(array, 0) + chunk + (everyone,) for array, chunk in zip(spread, CHUNKS)]
        tokens = (ids, tile_ids, windows)
        attended = attend(tokens, queries, pieces, everyone, [], start=begin, last=True, stacked=True)
    else:
        near = lambda values: lax.ppermute(values, "tiles", NEAR)
        away = lambda values: lax.ppermute(values, "tiles", AWAY)

        def piece(array, source, number, wanted):
            return (array, source) + CHUNKS[number] + (wanted,)

        query0, kv0 = project_chunk(0, (weight, parts[2]) if pairs else (), ())
        near0, away0 = near(kv0), away(kv0)
        query1, kv1 = project_chunk(1, (kv0,), ())
        both0 = near(ordered(away0, near0, kv1))
        near1, away1 = near(kv1), away(ordered(kv1, away0))
        labels = [array[CHUNKS[0][1], :per_dev].astype(jnp.int32) for array in (near0, away0)]
        early = (jnp.concatenate([tile_ids] + labels), tile_ids, windows)
        queries = [(0, query0), (CHUNKS[1][0], query1)]
        pieces = [piece(kv0, 0, 0, [0]), piece(kv1, 0, 1, [0])]
        pieces += [piece(near0, 1, 0, [0]), piece(away0, 2, 0, [0])]
        state = attend(early, queries, pieces, [0], [], start=begin)
        query2, kv2 = project_chunk(2, (kv1,), (state[1],))
        both1 = near(ordered(away1, near1, both0, kv2))
        near2, away2 = near(kv2), away(ordered(kv2, away1))
        labels.append(both0[CHUNKS[0][1], :per_dev].astype(jnp.int32))
        tokens = (jnp.concatenate([tile_ids] + labels), tile_ids, windows)
        queries.append((CHUNKS[2][0], query2))
        pieces = [piece(kv2, 0, 2, [0, 1]), piece(kv0, 0, 0, [1]), piece(kv1, 0, 1, [1])]
        pieces += [piece(near0, 1, 0, [1]), piece(away0, 2, 0, [1]), piece(both0, 3, 0, [0, 1])]
        pieces += [piece(near1, 1, 1, [0, 1]), piece(away1, 2, 1, [0, 1])]
        state = attend(tokens, queries, pieces, [1], [0], start=begin, state=state)
        both2 = near(ordered(away2, near2, both1, state[1]))
        pieces = [piece(both1, 3, 1, [0, 1]), piece(near2, 1, 2, [0, 1]), piece(away2, 2, 2, [0, 1])]
        state = attend(tokens, queries, pieces, [], [0, 1], state=state)
        attended = attend(tokens, queries, [piece(both2, 3, 2, [0, 1])], [], [0, 1], state=state, last=True)

    if pairs:
        far = shifted(attended, "heads", 2, 1)
        pieces = [attended, shifted(attended, "cfg", 2, 1), far, shifted(far, "cfg", 2, 1)]
    else:
        pieces = [lax.all_gather(attended, ("heads", "cfg"), axis=1, tiled=True)]
    gate = modulation if pairs else lax.dynamic_slice_in_dim(modulation[2:3], me * width, width, 1)
    return merge(places, pieces, proj_weight, latents, gate)


def solution(mesh):
    in_specs = (
        P(("groups", "tiles"), ("heads", "cfg")),
        P("groups", None),
        P(None, ("heads", "cfg")),
        P(),
        P(),
        P("groups", ("heads", "cfg")),
        P("groups"),
        P(("groups", "tiles")),
        P("groups", None),
        P(None, ("heads", "cfg")),
    )
    out_specs = P(("groups", "tiles"), ("heads", "cfg"))
    run = functools.partial(body, mesh.shape["heads"], mesh.shape["cfg"], mesh.shape["tiles"])
    return jax.shard_map(run, mesh=mesh, in_specs=in_specs, out_specs=out_specs, check_vma=False)
```

profile of v0, /device:TPU:0, one launch (start us, length us, event | category | flops | bytes accessed | tf_op | source)
XLA Modules:
  0.0 75.0 jit_solution(9999612608431097228)
XLA Ops:
  1.4 2.6 %collective-permute-start.1 = (bf16[128,768]{1,0:T(8,128)(2,1)S(1)}, bf16[128,768]{1,0:T(8,128)(2,1)}, u32[]{:S(2)}, u32[]{:S(2)}) collective-permute-start(bf16[128,768]{1,0:T(8,128)(2,1)S(1)} %slice.18), channel_id=1, source_target_pairs={{0,2},{2,0},{1,3},{3,1},{4,6},{6,4},{5,7},{7,5},{8,10},{10,8},{9,1... | collective-permute-start | bytes 589832 | tf_op jit(solution)/shard_map/ppermute | solution.py:284
  4.0 1.8 %slice.22 = bf16[256,768]{1,0:T(8,128)(2,1)} slice(bf16[768,768]{1,0:T(8,128)(2,1)} %refs_5_.3), slice={[128:384], [0:768]} | slice | bytes 786432 | tf_op jit(solution)/shard_map/slice | solution.py:327
  5.7 1.9 %slice.19 = bf16[384,768]{1,0:T(8,128)(2,1)} slice(bf16[768,768]{1,0:T(8,128)(2,1)} %refs_5_.3), slice={[384:768], [0:768]} | slice | bytes 1179648 | tf_op jit(solution)/shard_map/slice | solution.py:327
  7.7 1.7 %copy-done.1 = bf16[3072,384]{1,0:T(8,128)(2,1)S(1)} copy-done((bf16[3072,384]{1,0:T(8,128)(2,1)S(1)}, bf16[3072,384]{1,0:T(8,128)(2,1)}, u32[]{:S(2)}) %copy-start.1) | copy-done | bytes 2359320
  9.8 1.9 %collective-permute-start.8 = (bf16[384,768]{1,0:T(8,128)(2,1)}, bf16[384,768]{1,0:T(8,128)(2,1)}, u32[]{:S(2)}, u32[]{:S(2)}) collective-permute-start(bf16[384,768]{1,0:T(8,128)(2,1)} %slice.19), channel_id=1, source_target_pairs={{0,2},{2,0},{1,3},{3,1},{4,6},{6,4},{5,7},{7,5},{8,10},{10,8},{9,1... | collective-permute-start | bytes 1769480 | tf_op jit(solution)/shard_map/ppermute | solution.py:284
  12.7 3.0 %shard_map.101 = (bf16[128,128]{1,0:T(8,128)(2,1)S(1)}, bf16[144,256]{1,0:T(8,128)(2,1)S(1)}) custom-call(s32[4]{0:T(128)S(1)} %pad_add_fusion.place_ref, s32[2]{0:T(128)S(1)} %copy-done.7, bf16[768,768]{1,0:T(8,128)(2,1)S(1)} %copy-done, bf16[768,768]{1,0:T(8,128)(2,1)} %collective-permute-done.refs_1_, bf16[128,768]{1,0:T(8,128)(2,1)} %collective-permute-done.1.refs_2_, ...), custom_call_target="tpu_custom_call" | custom-call | flops 128 | bytes 128 | tf_op jit(solution)/shard_map/pallas_call | solution.py:104
  15.7 2.5 %collective-permute-done.5.refs_2_ = bf16[256,768]{1,0:T(8,128)(2,1)} collective-permute-done((bf16[256,768]{1,0:T(8,128)(2,1)}, bf16[256,768]{1,0:T(8,128)(2,1)}, u32[]{:S(2)}, u32[]{:S(2)}) %collective-permute-start.5) | collective-permute-done | bytes 393248 | tf_op jit(solution)/shard_map/ppermute | solution.py:284
  18.2 3.1 %collective-permute-start.4 = (bf16[144,256]{1,0:T(8,128)(2,1)S(1)}, bf16[144,256]{1,0:T(8,128)(2,1)S(1)}, u32[]{:S(2)}, u32[]{:S(2)}) collective-permute-start(bf16[144,256]{1,0:T(8,128)(2,1)S(1)} %get-tuple-element.31.refs_2_.refs_4_), channel_id=1, source_target_pairs={{0,8},{4,12},{8,0},{12,4},{1,9},{5,13},{9,1},{13,5},{2,10},{6,14},... | collective-permute-start | bytes 221192 | tf_op jit(solution)/shard_map/ppermute | solution.py:360
  21.4 3.7 %shard_map.102 = (bf16[256,128]{1,0:T(8,128)(2,1)S(1)}, bf16[256,256]{1,0:T(8,128)(2,1)S(1)}) custom-call(s32[4]{0:T(128)S(1)} %pad_add_fusion.place_ref, s32[2]{0:T(128)S(1)} %copy-done.7, bf16[768,768]{1,0:T(8,128)(2,1)S(1)} %copy-done, bf16[768,768]{1,0:T(8,128)(2,1)} %collective-permute-done.refs_1_, bf16[256,768]{1,0:T(8,128)(2,1)} %collective-permute-done.5.refs_2_, ...), custom_call_target="tpu_custom_call" | custom-call | flops 256 | bytes 256 | tf_op jit(solution)/shard_map/pallas_call | solution.py:104
  25.1 5.6 %collective-permute-done.8.refs_2_ = bf16[384,768]{1,0:T(8,128)(2,1)} collective-permute-done((bf16[384,768]{1,0:T(8,128)(2,1)}, bf16[384,768]{1,0:T(8,128)(2,1)}, u32[]{:S(2)}, u32[]{:S(2)}) %collective-permute-start.8) | collective-permute-done | bytes 589856 | tf_op jit(solution)/shard_map/ppermute | solution.py:284
  31.4 1.9 %collective-permute-start.3 = (bf16[144,256]{1,0:T(8,128)(2,1)S(1)}, bf16[144,256]{1,0:T(8,128)(2,1)S(1)}, u32[]{:S(2)}, u32[]{:S(2)}) collective-permute-start(bf16[144,256]{1,0:T(8,128)(2,1)S(1)} %get-tuple-element.31.refs_2_.refs_4_), channel_id=1, source_target_pairs={{0,4},{4,0},{8,12},{12,8},{1,5},{5,1},{9,13},{13,9},{2,6},{6,2},{1... | collective-permute-start | bytes 221192 | tf_op jit(solution)/shard_map/ppermute | solution.py:359
  33.5 2.8 %collective-permute-start.10 = (bf16[256,256]{1,0:T(8,128)(2,1)S(1)}, bf16[256,256]{1,0:T(8,128)(2,1)S(1)}, u32[]{:S(2)}, u32[]{:S(2)}) collective-permute-start(bf16[256,256]{1,0:T(8,128)(2,1)S(1)} %get-tuple-element.41.refs_3_.refs_5_), channel_id=1, source_target_pairs={{0,8},{4,12},{8,0},{12,4},{1,9},{5,13},{9,1},{13,5},{2,10},{6,14},... | collective-permute-start | bytes 393224 | tf_op jit(solution)/shard_map/ppermute | solution.py:360
  36.3 2.0 %collective-permute-start.7 = (bf16[144,256]{1,0:T(8,128)(2,1)S(1)}, bf16[144,256]{1,0:T(8,128)(2,1)S(1)}, u32[]{:S(2)}, u32[]{:S(2)}) collective-permute-start(bf16[144,256]{1,0:T(8,128)(2,1)S(1)} %collective-permute-done.4.refs_5_.refs_7_), channel_id=1, source_target_pairs={{0,4},{4,0},{8,12},{12,8},{1,5},{5,1},{9,13},{13,9},{2,6},{6,2},{1... | collective-permute-start | bytes 221192 | tf_op jit(solution)/shard_map/ppermute | solution.py:359
  38.4 2.1 %shard_map.103 = (f32[768,128]{1,0:T(8,128)S(1)}, f32[768,128]{1,0:T(8,128)S(1)}, f32[768,128]{1,0:T(8,128)S(1)}) custom-call(s32[6]{0:T(128)S(1)} %pad_add_fusion.2.ids_ref, s32[2]{0:T(128)S(1)} %copy-done.7, s32[8,27]{1,0:T(8,128)S(1)} %copy-done.6, bf16[128,128]{1,0:T(8,128)(2,1)S(1)} %get-tuple-element.35.refs_0_, ...), custom_call_target="tpu_custom_call" | custom-call | flops 528384 | bytes 98304 | tf_op jit(solution)/shard_map/pallas_call | solution.py:225
  40.5 4.4 %shard_map.104 = (bf16[384,128]{1,0:T(8,128)(2,1)S(1)}, bf16[384,256]{1,0:T(8,128)(2,1)S(1)}) custom-call(s32[4]{0:T(128)S(1)} %pad_add_fusion.place_ref, s32[2]{0:T(128)S(1)} %copy-done.7, bf16[768,768]{1,0:T(8,128)(2,1)S(1)} %copy-done, bf16[768,768]{1,0:T(8,128)(2,1)} %collective-permute-done.refs_1_, bf16[384,768]{1,0:T(8,128)(2,1)} %collective-permute-done.8.refs_2_, ...), custom_call_target="tpu_custom_call" | custom-call | flops 384 | bytes 384 | tf_op jit(solution)/shard_map/pallas_call | solution.py:104
  45.0 2.6 %collective-permute-start.11 = (bf16[384,256]{1,0:T(8,128)(2,1)S(1)}, bf16[384,256]{1,0:T(8,128)(2,1)S(1)}, u32[]{:S(2)}, u32[]{:S(2)}) collective-permute-start(bf16[384,256]{1,0:T(8,128)(2,1)S(1)} %get-tuple-element.42.refs_3_), channel_id=1, source_target_pairs={{0,8},{4,12},{8,0},{12,4},{1,9},{5,13},{9,1},{13,5},{2,10},{6,14},... | collective-permute-start | bytes 589832 | tf_op jit(solution)/shard_map/ppermute | solution.py:360
  47.6 1.7 %collective-permute-start.14 = (bf16[256,256]{1,0:T(8,128)(2,1)S(1)}, bf16[256,256]{1,0:T(8,128)(2,1)S(1)}, u32[]{:S(2)}, u32[]{:S(2)}) collective-permute-start(bf16[256,256]{1,0:T(8,128)(2,1)S(1)} %collective-permute-done.10.refs_10_), channel_id=1, source_target_pairs={{0,4},{4,0},{8,12},{12,8},{1,5},{5,1},{9,13},{13,9},{2,6},{6,2},{1... | collective-permute-start | bytes 393224 | tf_op jit(solution)/shard_map/ppermute | solution.py:359
  49.4 3.8 %shard_map.105 = (f32[768,128]{1,0:T(8,128)S(1)}, f32[768,128]{1,0:T(8,128)S(1)}, f32[768,128]{1,0:T(8,128)S(1)}) custom-call(s32[8]{0:T(128)S(1)} %pad_add_fusion.1.ids_ref, s32[2]{0:T(128)S(1)} %copy-done.7, s32[8,27]{1,0:T(8,128)S(1)} %copy-done.6, bf16[128,128]{1,0:T(8,128)(2,1)S(1)} %get-tuple-element.35.refs_0_, ...), custom_call_target="tpu_custom_call" | custom-call | flops 1327104 | bytes 98304 | tf_op jit(solution)/shard_map/pallas_call | solution.py:225
  53.1 4.7 %collective-permute-done.14.refs_3_ = bf16[256,256]{1,0:T(8,128)(2,1)S(1)} collective-permute-done((bf16[256,256]{1,0:T(8,128)(2,1)S(1)}, bf16[256,256]{1,0:T(8,128)(2,1)S(1)}, u32[]{:S(2)}, u32[]{:S(2)}) %collective-permute-start.14) | collective-permute-done | bytes 131104 | tf_op jit(solution)/shard_map/ppermute | solution.py:359
  58.7 2.3 %shard_map.106 = (f32[768,128]{1,0:T(8,128)S(1)}, f32[768,128]{1,0:T(8,128)S(1)}, f32[768,128]{1,0:T(8,128)S(1)}) custom-call(s32[8]{0:T(128)S(1)} %pad_add_fusion.1.ids_ref, s32[2]{0:T(128)S(1)} %copy-done.7, s32[8,27]{1,0:T(8,128)S(1)} %copy-done.6, bf16[128,128]{1,0:T(8,128)(2,1)S(1)} %get-tuple-element.35.refs_0_, ...), custom_call_target="tpu_custom_call" | custom-call | flops 786432 | bytes 98304 | tf_op jit(solution)/shard_map/pallas_call | solution.py:225
  61.0 2.6 %collective-permute-done.15.refs_3_ = bf16[384,256]{1,0:T(8,128)(2,1)S(1)} collective-permute-done((bf16[384,256]{1,0:T(8,128)(2,1)S(1)}, bf16[384,256]{1,0:T(8,128)(2,1)S(1)}, u32[]{:S(2)}, u32[]{:S(2)}) %collective-permute-start.15) | collective-permute-done | bytes 196640 | tf_op jit(solution)/shard_map/ppermute | solution.py:359
  65.0 1.6 %collective-permute-start.17 = (bf16[768,128]{1,0:T(8,128)(2,1)S(1)}, bf16[768,128]{1,0:T(8,128)(2,1)S(1)}, u32[]{:S(2)}, u32[]{:S(2)}) collective-permute-start(bf16[768,128]{1,0:T(8,128)(2,1)S(1)} %shard_map.107.refs_0_), channel_id=1, source_target_pairs={{0,2},{2,0},{1,3},{3,1},{4,6},{6,4},{5,7},{7,5},{8,10},{10,8},{9,1... | collective-permute-start | bytes 589832 | tf_op jit(solution)/shard_map/ppermute | solution.py:284
  66.5 4.2 %collective-permute-done.17.refs_2_ = bf16[768,128]{1,0:T(8,128)(2,1)S(1)} collective-permute-done((bf16[768,128]{1,0:T(8,128)(2,1)S(1)}, bf16[768,128]{1,0:T(8,128)(2,1)S(1)}, u32[]{:S(2)}, u32[]{:S(2)}) %collective-permute-start.17) | collective-permute-done | bytes 196640 | tf_op jit(solution)/shard_map/ppermute | solution.py:284
  72.2 2.8 %shard_map.108 = bf16[768,768]{1,0:T(8,128)(2,1)} custom-call(s32[4]{0:T(128)S(1)} %pad_add_fusion.place_ref, bf16[768,128]{1,0:T(8,128)(2,1)S(1)} %shard_map.107.refs_0_, bf16[768,128]{1,0:T(8,128)(2,1)S(1)} %collective-permute-done.16.refs_1_, bf16[768,128]{1,0:T(8,128)(2,1)S(1)} %collective-permute-done.17.refs_2_, ...), custom_call_target="tpu_custom_call" | custom-call | flops 603979776 | bytes 3932160 | tf_op jit(solution)/shard_map/pallas_call | solution.py:261
  (52 shorter events, 6.9 us)
Async XLA Ops:
  0.0 11.8 %collective-permute-start = (bf16[768,768]{1,0:T(8,128)(2,1)}, bf16[768,768]{1,0:T(8,128)(2,1)}, u32[]{:S(2)}, u32[]{:S(2)}) collective-permute-start(bf16[768,768]{1,0:T(8,128)(2,1)} %refs_5_.3), channel_id=1, source_target_pairs={{0,1},{1,0},{2,3},{3,2},{4,5},{5,4},{6,7},{7,6},{8,9},{9,8},{10,11... | collective-permute-start | bytes 3538952 | tf_op jit(solution)/shard_map/ppermute | solution.py:284
  1.4 8.4 %collective-permute-start.1 = (bf16[128,768]{1,0:T(8,128)(2,1)S(1)}, bf16[128,768]{1,0:T(8,128)(2,1)}, u32[]{:S(2)}, u32[]{:S(2)}) collective-permute-start(bf16[128,768]{1,0:T(8,128)(2,1)S(1)} %slice.18), channel_id=1, source_target_pairs={{0,2},{2,0},{1,3},{3,1},{4,6},{6,4},{5,7},{7,5},{8,10},{10,8},{9,1... | collective-permute-start | bytes 589832 | tf_op jit(solution)/shard_map/ppermute | solution.py:284
  5.7 12.5 %collective-permute-start.5 = (bf16[256,768]{1,0:T(8,128)(2,1)}, bf16[256,768]{1,0:T(8,128)(2,1)}, u32[]{:S(2)}, u32[]{:S(2)}) collective-permute-start(bf16[256,768]{1,0:T(8,128)(2,1)} %slice.22), channel_id=1, source_target_pairs={{0,2},{2,0},{1,3},{3,1},{4,6},{6,4},{5,7},{7,5},{8,10},{10,8},{9,1... | collective-permute-start | bytes 1179656 | tf_op jit(solution)/shard_map/ppermute | solution.py:284
  9.3 2.5 %copy-start.9 = (f32[128]{0:T(128)S(1)}, f32[128]{0:T(128)}, u32[]{:S(2)}) copy-start(f32[128]{0:T(128)} %param.14) | copy-start | bytes 1540
  9.8 2.0 %collective-permute-start.2 = (bf16[128,768]{1,0:T(8,128)(2,1)}, bf16[128,768]{1,0:T(8,128)(2,1)}, u32[]{:S(2)}, u32[]{:S(2)}) collective-permute-start(bf16[128,768]{1,0:T(8,128)(2,1)} %collective-permute-done.1.refs_2_), channel_id=1, source_target_pairs={{0,1},{1,0},{2,3},{3,2},{4,5},{5,4},{6,7},{7,6},{8,9},{9,8},{10,11... | collective-permute-start | bytes 589832 | tf_op jit(solution)/shard_map/ppermute | solution.py:284
  9.8 20.9 %collective-permute-start.8 = (bf16[384,768]{1,0:T(8,128)(2,1)}, bf16[384,768]{1,0:T(8,128)(2,1)}, u32[]{:S(2)}, u32[]{:S(2)}) collective-permute-start(bf16[384,768]{1,0:T(8,128)(2,1)} %slice.19), channel_id=1, source_target_pairs={{0,2},{2,0},{1,3},{3,1},{4,6},{6,4},{5,7},{7,5},{8,10},{10,8},{9,1... | collective-permute-start | bytes 1769480 | tf_op jit(solution)/shard_map/ppermute | solution.py:284
  12.7 8.7 %copy-start.3 = (f32[3,3072]{1,0:T(4,128)S(1)}, f32[3,3072]{1,0:T(4,128)}, u32[]{:S(2)}) copy-start(f32[3,3072]{1,0:T(4,128)} %refs_6_.2) | copy-start | bytes 110596
  18.2 20.2 %copy-start.5 = (bf16[256,256]{1,0:T(8,128)(2,1)S(1)}, bf16[256,256]{1,0:T(8,128)(2,1)}, u32[]{:S(2)}) copy-start(bf16[256,256]{1,0:T(8,128)(2,1)} %refs_12_.1) | copy-start | bytes 393220
  18.2 20.2 %copy-start.6 = (s32[8,27]{1,0:T(8,128)S(1)}, s32[8,27]{1,0:T(8,128)}, u32[]{:S(2)}) copy-start(s32[8,27]{1,0:T(8,128)} %windows_ref.7) | copy-start | bytes 2596
  18.2 3.1 %collective-permute-start.6 = (bf16[256,768]{1,0:T(8,128)(2,1)}, bf16[256,768]{1,0:T(8,128)(2,1)S(1)}, u32[]{:S(2)}, u32[]{:S(2)}) collective-permute-start(bf16[256,768]{1,0:T(8,128)(2,1)} %collective-permute-done.5.refs_2_), channel_id=1, source_target_pairs={{0,1},{1,0},{2,3},{3,2},{4,5},{5,4},{6,7},{7,6},{8,9},{9,8},{10,11... | collective-permute-start | bytes 1179656 | tf_op jit(solution)/shard_map/ppermute | solution.py:284
  18.2 15.0 %collective-permute-start.4 = (bf16[144,256]{1,0:T(8,128)(2,1)S(1)}, bf16[144,256]{1,0:T(8,128)(2,1)S(1)}, u32[]{:S(2)}, u32[]{:S(2)}) collective-permute-start(bf16[144,256]{1,0:T(8,128)(2,1)S(1)} %get-tuple-element.31.refs_2_.refs_4_), channel_id=1, source_target_pairs={{0,8},{4,12},{8,0},{12,4},{1,9},{5,13},{9,1},{13,5},{2,10},{6,14},... | collective-permute-start | bytes 221192 | tf_op jit(solution)/shard_map/ppermute | solution.py:360
  30.7 9.8 %collective-permute-start.9 = (bf16[384,768]{1,0:T(8,128)(2,1)}, bf16[384,768]{1,0:T(8,128)(2,1)S(1)}, u32[]{:S(2)}, u32[]{:S(2)}) collective-permute-start(bf16[384,768]{1,0:T(8,128)(2,1)} %collective-permute-done.8.refs_2_), channel_id=1, source_target_pairs={{0,1},{1,0},{2,3},{3,2},{4,5},{5,4},{6,7},{7,6},{8,9},{9,8},{10,11... | collective-permute-start | bytes 1769480 | tf_op jit(solution)/shard_map/ppermute | solution.py:284
  31.4 4.9 %collective-permute-start.3 = (bf16[144,256]{1,0:T(8,128)(2,1)S(1)}, bf16[144,256]{1,0:T(8,128)(2,1)S(1)}, u32[]{:S(2)}, u32[]{:S(2)}) collective-permute-start(bf16[144,256]{1,0:T(8,128)(2,1)S(1)} %get-tuple-element.31.refs_2_.refs_4_), channel_id=1, source_target_pairs={{0,4},{4,0},{8,12},{12,8},{1,5},{5,1},{9,13},{13,9},{2,6},{6,2},{1... | collective-permute-start | bytes 221192 | tf_op jit(solution)/shard_map/ppermute | solution.py:359
  33.3 14.4 %collective-permute-start.13 = (bf16[256,256]{1,0:T(8,128)(2,1)S(1)}, bf16[256,256]{1,0:T(8,128)(2,1)S(1)}, u32[]{:S(2)}, u32[]{:S(2)}) collective-permute-start(bf16[256,256]{1,0:T(8,128)(2,1)S(1)} %get-tuple-element.41.refs_3_.refs_5_), channel_id=1, source_target_pairs={{0,4},{4,0},{8,12},{12,8},{1,5},{5,1},{9,13},{13,9},{2,6},{6,2},{1... | collective-permute-start | bytes 393224 | tf_op jit(solution)/shard_map/ppermute | solution.py:359
  33.5 11.5 %collective-permute-start.10 = (bf16[256,256]{1,0:T(8,128)(2,1)S(1)}, bf16[256,256]{1,0:T(8,128)(2,1)S(1)}, u32[]{:S(2)}, u32[]{:S(2)}) collective-permute-start(bf16[256,256]{1,0:T(8,128)(2,1)S(1)} %get-tuple-element.41.refs_3_.refs_5_), channel_id=1, source_target_pairs={{0,8},{4,12},{8,0},{12,4},{1,9},{5,13},{9,1},{13,5},{2,10},{6,14},... | collective-permute-start | bytes 393224 | tf_op jit(solution)/shard_map/ppermute | solution.py:360
  36.3 11.3 %collective-permute-start.7 = (bf16[144,256]{1,0:T(8,128)(2,1)S(1)}, bf16[144,256]{1,0:T(8,128)(2,1)S(1)}, u32[]{:S(2)}, u32[]{:S(2)}) collective-permute-start(bf16[144,256]{1,0:T(8,128)(2,1)S(1)} %collective-permute-done.4.refs_5_.refs_7_), channel_id=1, source_target_pairs={{0,4},{4,0},{8,12},{12,8},{1,5},{5,1},{9,13},{13,9},{2,6},{6,2},{1... | collective-permute-start | bytes 221192 | tf_op jit(solution)/shard_map/ppermute | solution.py:359
  44.9 13.0 %collective-permute-start.12 = (bf16[384,256]{1,0:T(8,128)(2,1)S(1)}, bf16[384,256]{1,0:T(8,128)(2,1)S(1)}, u32[]{:S(2)}, u32[]{:S(2)}) collective-permute-start(bf16[384,256]{1,0:T(8,128)(2,1)S(1)} %get-tuple-element.42.refs_3_), channel_id=1, source_target_pairs={{0,4},{4,0},{8,12},{12,8},{1,5},{5,1},{9,13},{13,9},{2,6},{6,2},{1... | collective-permute-start | bytes 589832 | tf_op jit(solution)/shard_map/ppermute | solution.py:359
  45.0 12.9 %collective-permute-start.11 = (bf16[384,256]{1,0:T(8,128)(2,1)S(1)}, bf16[384,256]{1,0:T(8,128)(2,1)S(1)}, u32[]{:S(2)}, u32[]{:S(2)}) collective-permute-start(bf16[384,256]{1,0:T(8,128)(2,1)S(1)} %get-tuple-element.42.refs_3_), channel_id=1, source_target_pairs={{0,8},{4,12},{8,0},{12,4},{1,9},{5,13},{9,1},{13,5},{2,10},{6,14},... | collective-permute-start | bytes 589832 | tf_op jit(solution)/shard_map/ppermute | solution.py:360
  47.6 10.3 %collective-permute-start.14 = (bf16[256,256]{1,0:T(8,128)(2,1)S(1)}, bf16[256,256]{1,0:T(8,128)(2,1)S(1)}, u32[]{:S(2)}, u32[]{:S(2)}) collective-permute-start(bf16[256,256]{1,0:T(8,128)(2,1)S(1)} %collective-permute-done.10.refs_10_), channel_id=1, source_target_pairs={{0,4},{4,0},{8,12},{12,8},{1,5},{5,1},{9,13},{13,9},{2,6},{6,2},{1... | collective-permute-start | bytes 393224 | tf_op jit(solution)/shard_map/ppermute | solution.py:359
  57.9 5.8 %collective-permute-start.15 = (bf16[384,256]{1,0:T(8,128)(2,1)S(1)}, bf16[384,256]{1,0:T(8,128)(2,1)S(1)}, u32[]{:S(2)}, u32[]{:S(2)}) collective-permute-start(bf16[384,256]{1,0:T(8,128)(2,1)S(1)} %collective-permute-done.11.refs_5_), channel_id=1, source_target_pairs={{0,4},{4,0},{8,12},{12,8},{1,5},{5,1},{9,13},{13,9},{2,6},{6,2},{1... | collective-permute-start | bytes 589832 | tf_op jit(solution)/shard_map/ppermute | solution.py:359
  61.0 11.1 %copy-start.4 = (bf16[512,768]{1,0:T(8,128)(2,1)S(1)}, bf16[512,768]{1,0:T(8,128)(2,1)}, u32[]{:S(2)}) copy-start(bf16[512,768]{1,0:T(8,128)(2,1)} %refs_4_.5) | copy-start | bytes 2359300
  65.0 5.7 %collective-permute-start.17 = (bf16[768,128]{1,0:T(8,128)(2,1)S(1)}, bf16[768,128]{1,0:T(8,128)(2,1)S(1)}, u32[]{:S(2)}, u32[]{:S(2)}) collective-permute-start(bf16[768,128]{1,0:T(8,128)(2,1)S(1)} %shard_map.107.refs_0_), channel_id=1, source_target_pairs={{0,2},{2,0},{1,3},{3,1},{4,6},{6,4},{5,7},{7,5},{8,10},{10,8},{9,1... | collective-permute-start | bytes 589832 | tf_op jit(solution)/shard_map/ppermute | solution.py:284
  66.5 4.2 %collective-permute-start.16 = (bf16[768,128]{1,0:T(8,128)(2,1)S(1)}, bf16[768,128]{1,0:T(8,128)(2,1)S(1)}, u32[]{:S(2)}, u32[]{:S(2)}) collective-permute-start(bf16[768,128]{1,0:T(8,128)(2,1)S(1)} %shard_map.107.refs_0_), channel_id=1, source_target_pairs={{0,1},{1,0},{2,3},{3,2},{4,5},{5,4},{6,7},{7,6},{8,9},{9,8},{10,11... | collective-permute-start | bytes 589832 | tf_op jit(solution)/shard_map/ppermute | solution.py:284
  70.7 1.4 %collective-permute-start.18 = (bf16[768,128]{1,0:T(8,128)(2,1)S(1)}, bf16[768,128]{1,0:T(8,128)(2,1)S(1)}, u32[]{:S(2)}, u32[]{:S(2)}) collective-permute-start(bf16[768,128]{1,0:T(8,128)(2,1)S(1)} %collective-permute-done.17.refs_2_), channel_id=1, source_target_pairs={{0,1},{1,0},{2,3},{3,2},{4,5},{5,4},{6,7},{7,6},{8,9},{9,8},{10,11... | collective-permute-start | bytes 589832 | tf_op jit(solution)/shard_map/ppermute | solution.py:284
  (5 other events, 10.0 us)
where the time goes:
time: 75.6 us; the launch traced here: 75 us
  Pallas kernels  23.6 us (31%)
  starting transfers between devices  21.8 us (29%)
  waiting for transfers between devices  21.5 us (28%)
  local copies, waits for them, and re-layouts  7.11 us (9%)
  between operations  0.82 us (1%)
    ppermute x10, waiting for transfers between devices, shifted(): lax.ppermute(values, axis, [(at, (at + by) % size) for at in range(size)])  14.1 us
    pallas_call x3, Pallas kernels, project(): pl.pallas_call(functools.partial(project_kernel, count, len(after), start...  11.1 us
    pallas_call x4, Pallas kernels, attend(): pl.pallas_call(functools.partial(attend_kernel, [at for at, array in quer...  9.43 us
    ppermute x3, starting transfers between devices, body(): away = lambda values: lax.ppermute(values, 'tiles', AWAY)  8.54 us
    ppermute x6, waiting for transfers between devices, body(): near = lambda values: lax.ppermute(values, 'tiles', NEAR)  7.34 us
    ppermute x6, starting transfers between devices, body(): near = lambda values: lax.ppermute(values, 'tiles', NEAR)  6.71 us
    ppermute x10, starting transfers between devices, shifted(): lax.ppermute(values, axis, [(at, (at + by) % size) for at in range(size)])  6.54 us
    slice x2, local copies, waits for them, and re-layouts, body(): parts += [rest[start:start + size] for start, size in CHUNKS[1:]]  3.68 us
  transfers between devices with their start and end apart: 19, of which 7 were waited for; matrix products, arithmetic and copies ran while one was open for 6% of the time, Pallas kernels for 26%

commit v1 on v0

--- a/solution.py
+++ b/solution.py
@@ -238,39 +238,42 @@
     )(ids, own_ids, windows, *[array for at, array in queries], *[piece[0] for piece in pieces], *extra)
 
 
-def merge_kernel(count, place_ref, *refs):
+def merge_kernel(count, block, place_ref, *refs):
     pieces = refs[:count]
-    weight_ref, latents_ref, gate_ref, out_ref, joined_ref = refs[count:]
+    weight_ref, latents_ref, gate_ref, out_ref, joined_ref, made_ref, sem = refs[count:]
     depth = pieces[0].shape[1]
     width = latents_ref.shape[1]
     if count > 1:
         gate = gate_ref[2:3, pl.ds(pl.multiple_of(place_ref[0] * width, width), width)]
         for place, piece in enumerate(pieces):
             joined_ref[:, pl.ds(pl.multiple_of(place_ref[place] * depth, depth), depth)] = piece[...]
-        attended = joined_ref[...]
     else:
         gate = gate_ref[...]
-        attended = pieces[0][...]
-    product = jnp.dot(attended, weight_ref[...], preferred_element_type=jnp.float32)
-    out_ref[...] = (latents_ref[...].astype(jnp.float32) + gate * product).astype(jnp.bfloat16)
+        joined_ref[...] = pieces[0][...]
+    copies = []
+    for number in range(latents_ref.shape[0] // block):
+        rows = slice(number * block, (number + 1) * block)
+        product = jnp.dot(joined_ref[rows, :], weight_ref[...], preferred_element_type=jnp.float32)
+        made_ref[rows, :] = (latents_ref[rows, :].astype(jnp.float32) + gate * product).astype(jnp.bfloat16)
+        copies.append(pltpu.make_async_copy(made_ref.at[rows, :], out_ref.at[rows, :], sem.at[number]))
+        copies[-1].start()
+    for copy in copies:
+        copy.wait()
 
 
 def merge(places, pieces, weight, latents, gate):
     rows, width = latents.shape
     block = 256
     return pl.pallas_call(
-        functools.partial(merge_kernel, len(pieces)),
-        grid=(rows // block,),
+        functools.partial(merge_kernel, len(pieces), block),
         out_shape=jax.ShapeDtypeStruct((rows, width), jnp.bfloat16),
-        in_specs=[SMEM]
-        + [pl.BlockSpec((block, piece.shape[1]), lambda i: (i, 0)) for piece in pieces]
-        + [
-            pl.BlockSpec(weight.shape, lambda i: (0, 0)),
-            pl.BlockSpec((block, width), lambda i: (i, 0)),
-            pl.BlockSpec(gate.shape, lambda i: (0, 0)),
+        in_specs=[SMEM] + [VMEM] * (len(pieces) + 3),
+        out_specs=HBM,
+        scratch_shapes=[
+            pltpu.VMEM((rows, weight.shape[0]), jnp.bfloat16),
+            pltpu.VMEM((rows, width), jnp.bfloat16),
+            pltpu.SemaphoreType.DMA((rows // block,)),
         ],
-        out_specs=pl.BlockSpec((block, width), lambda i: (i, 0)),
-        scratch_shapes=[pltpu.VMEM((block, len(pieces) * pieces[0].shape[1]), jnp.bfloat16)],
         compiler_params=pltpu.CompilerParams(vmem_limit_bytes=MERGE_LIMIT),
         cost_estimate=pl.CostEstimate(
             flops=2 * rows * width * weight.shape[0],
@@ -371,16 +374,15 @@
         early = (jnp.concatenate([tile_ids] + labels), tile_ids, windows)
         queries = [(0, query0), (CHUNKS[1][0], query1)]
         pieces = [piece(kv0, 0, 0, [0]), piece(kv1, 0, 1, [0])]
-        pieces += [piece(near0, 1, 0, [0]), piece(away0, 2, 0, [0])]
-        state = attend(early, queries, pieces, [0], [], start=begin)
-        query2, kv2 = project_chunk(2, (kv1,), (state[1],))
+        state = attend((tile_ids, tile_ids, windows), queries, pieces, [0], [], start=begin)
+        query2, kv2 = project_chunk(2, (kv1, state[1], near0, away0), ())
         both1 = near(ordered(away1, near1, both0, kv2))
         near2, away2 = near(kv2), away(ordered(kv2, away1))
         labels.append(both0[CHUNKS[0][1], :per_dev].astype(jnp.int32))
         tokens = (jnp.concatenate([tile_ids] + labels), tile_ids, windows)
         queries.append((CHUNKS[2][0], query2))
         pieces = [piece(kv2, 0, 2, [0, 1]), piece(kv0, 0, 0, [1]), piece(kv1, 0, 1, [1])]
-        pieces += [piece(near0, 1, 0, [1]), piece(away0, 2, 0, [1]), piece(both0, 3, 0, [0, 1])]
+        pieces += [piece(near0, 1, 0, [0, 1]), piece(away0, 2, 0, [0, 1]), piece(both0, 3, 0, [0, 1])]
         pieces += [piece(near1, 1, 1, [0, 1]), piece(away1, 2, 1, [0, 1])]
         state = attend(tokens, queries, pieces, [1], [0], start=begin, state=state)
         both2 = near(ordered(away2, near2, both1, state[1]))

time: 75.6 us -> 70.6 us (0.934)
  waiting for transfers between devices: 21.5 us -> 15.9 us
  starting transfers between devices: 21.8 us -> 24 us
  Pallas kernels: 23.6 us -> 22.4 us
    ppermute x10, waiting for transfers between devices: 14.1 us -> 10.5 us  [shifted(): lax.ppermute(values, axis, [(at, (at + by) % size) for at in range(size)])]
    ppermute x6, starting transfers between devices: 6.71 us -> 9.46 us  [body(): near = lambda values: lax.ppermute(values, 'tiles', NEAR)]
    ppermute x6, waiting for transfers between devices: 7.34 us -> 5.46 us  [body(): near = lambda values: lax.ppermute(values, 'tiles', NEAR)]
  transfers between devices with their start and end apart: 19 -> 19, of which waited for: 7 -> 7; matrix products, arithmetic and copies ran while one was open for 6% -> 7% of each run, Pallas kernels for 26% -> 26%
where the time goes in v1:
time: 70.6 us; the launch traced here: 70.4 us
  starting transfers between devices  24 us (34%)
  Pallas kernels  22.4 us (32%)
  waiting for transfers between devices  15.9 us (23%)
  local copies, waits for them, and re-layouts  7.12 us (10%)
  between operations  0.85 us (1%)
    pallas_call x3, Pallas kernels, project(): pl.pallas_call(functools.partial(project_kernel, count, len(after), start...  11.1 us
    ppermute x10, waiting for transfers between devices, shifted(): lax.ppermute(values, axis, [(at, (at + by) % size) for at in range(size)])  10.5 us
    ppermute x6, starting transfers between devices, body(): near = lambda values: lax.ppermute(values, 'tiles', NEAR)  9.46 us
    pallas_call x4, Pallas kernels, attend(): pl.pallas_call(functools.partial(attend_kernel, [at for at, array in quer...  8.81 us
    ppermute x3, starting transfers between devices, body(): away = lambda values: lax.ppermute(values, 'tiles', AWAY)  7.98 us
    ppermute x10, starting transfers between devices, shifted(): lax.ppermute(values, axis, [(at, (at + by) % size) for at in range(size)])  6.56 us
    ppermute x6, waiting for transfers between devices, body(): near = lambda values: lax.ppermute(values, 'tiles', NEAR)  5.46 us
    slice x2, local copies, waits for them, and re-layouts, body(): parts += [rest[start:start + size] for start, size in CHUNKS[1:]]  3.68 us
  transfers between devices with their start and end apart: 19, of which 7 were waited for; matrix products, arithmetic and copies ran while one was open for 7% of the time, Pallas kernels for 26%

profile of v1, /device:TPU:0, one launch (start us, length us, event | category | flops | bytes accessed | tf_op | source)
XLA Modules:
  0.0 70.4 jit_solution(6727030636551656766)
XLA Ops:
  1.4 2.6 %collective-permute-start.1 = (bf16[128,768]{1,0:T(8,128)(2,1)S(1)}, bf16[128,768]{1,0:T(8,128)(2,1)}, u32[]{:S(2)}, u32[]{:S(2)}) collective-permute-start(bf16[128,768]{1,0:T(8,128)(2,1)S(1)} %slice.18), channel_id=1, source_target_pairs={{0,2},{2,0},{1,3},{3,1},{4,6},{6,4},{5,7},{7,5},{8,10},{10,8},{9,1... | collective-permute-start | bytes 589832 | tf_op jit(solution)/shard_map/ppermute | solution.py:287
  4.0 1.8 %slice.22 = bf16[256,768]{1,0:T(8,128)(2,1)} slice(bf16[768,768]{1,0:T(8,128)(2,1)} %refs_5_.3), slice={[128:384], [0:768]} | slice | bytes 786432 | tf_op jit(solution)/shard_map/slice | solution.py:330
  5.7 1.9 %slice.19 = bf16[384,768]{1,0:T(8,128)(2,1)} slice(bf16[768,768]{1,0:T(8,128)(2,1)} %refs_5_.3), slice={[384:768], [0:768]} | slice | bytes 1179648 | tf_op jit(solution)/shard_map/slice | solution.py:330
  7.7 1.7 %copy-done.1 = bf16[3072,384]{1,0:T(8,128)(2,1)S(1)} copy-done((bf16[3072,384]{1,0:T(8,128)(2,1)S(1)}, bf16[3072,384]{1,0:T(8,128)(2,1)}, u32[]{:S(2)}) %copy-start.1) | copy-done | bytes 2359320
  9.8 1.9 %collective-permute-start.8 = (bf16[384,768]{1,0:T(8,128)(2,1)}, bf16[384,768]{1,0:T(8,128)(2,1)}, u32[]{:S(2)}, u32[]{:S(2)}) collective-permute-start(bf16[384,768]{1,0:T(8,128)(2,1)} %slice.19), channel_id=1, source_target_pairs={{0,2},{2,0},{1,3},{3,1},{4,6},{6,4},{5,7},{7,5},{8,10},{10,8},{9,1... | collective-permute-start | bytes 1769480 | tf_op jit(solution)/shard_map/ppermute | solution.py:287
  12.7 3.0 %shard_map.101 = (bf16[128,128]{1,0:T(8,128)(2,1)S(1)}, bf16[144,256]{1,0:T(8,128)(2,1)S(1)}) custom-call(s32[4]{0:T(128)S(1)} %pad_add_fusion.place_ref, s32[2]{0:T(128)S(1)} %copy-done.7, bf16[768,768]{1,0:T(8,128)(2,1)S(1)} %copy-done, bf16[768,768]{1,0:T(8,128)(2,1)} %collective-permute-done.refs_1_, bf16[128,768]{1,0:T(8,128)(2,1)} %collective-permute-done.1.refs_2_, ...), custom_call_target="tpu_custom_call" | custom-call | flops 128 | bytes 128 | tf_op jit(solution)/shard_map/pallas_call | solution.py:104
  15.7 2.5 %collective-permute-done.5.refs_2_ = bf16[256,768]{1,0:T(8,128)(2,1)} collective-permute-done((bf16[256,768]{1,0:T(8,128)(2,1)}, bf16[256,768]{1,0:T(8,128)(2,1)}, u32[]{:S(2)}, u32[]{:S(2)}) %collective-permute-start.5) | collective-permute-done | bytes 393248 | tf_op jit(solution)/shard_map/ppermute | solution.py:287
  18.2 3.0 %collective-permute-start.4 = (bf16[144,256]{1,0:T(8,128)(2,1)S(1)}, bf16[144,256]{1,0:T(8,128)(2,1)S(1)}, u32[]{:S(2)}, u32[]{:S(2)}) collective-permute-start(bf16[144,256]{1,0:T(8,128)(2,1)S(1)} %get-tuple-element.31.refs_2_.refs_4_), channel_id=1, source_target_pairs={{0,8},{4,12},{8,0},{12,4},{1,9},{5,13},{9,1},{13,5},{2,10},{6,14},... | collective-permute-start | bytes 221192 | tf_op jit(solution)/shard_map/ppermute | solution.py:363
  23.6 3.7 %shard_map.102 = (bf16[256,128]{1,0:T(8,128)(2,1)S(1)}, bf16[256,256]{1,0:T(8,128)(2,1)S(1)}) custom-call(s32[4]{0:T(128)S(1)} %pad_add_fusion.place_ref, s32[2]{0:T(128)S(1)} %copy-done.7, bf16[768,768]{1,0:T(8,128)(2,1)S(1)} %copy-done, bf16[768,768]{1,0:T(8,128)(2,1)} %collective-permute-done.refs_1_, bf16[256,768]{1,0:T(8,128)(2,1)} %collective-permute-done.5.refs_2_, ...), custom_call_target="tpu_custom_call" | custom-call | flops 256 | bytes 256 | tf_op jit(solution)/shard_map/pallas_call | solution.py:104
  28.7 2.0 %collective-permute-done.8.refs_2_ = bf16[384,768]{1,0:T(8,128)(2,1)} collective-permute-done((bf16[384,768]{1,0:T(8,128)(2,1)}, bf16[384,768]{1,0:T(8,128)(2,1)}, u32[]{:S(2)}, u32[]{:S(2)}) %collective-permute-start.8) | collective-permute-done | bytes 589856 | tf_op jit(solution)/shard_map/ppermute | solution.py:287
  30.7 1.9 %collective-permute-start.13 = (bf16[256,256]{1,0:T(8,128)(2,1)S(1)}, bf16[256,256]{1,0:T(8,128)(2,1)S(1)}, u32[]{:S(2)}, u32[]{:S(2)}) collective-permute-start(bf16[256,256]{1,0:T(8,128)(2,1)S(1)} %get-tuple-element.41.refs_3_.refs_5_), channel_id=1, source_target_pairs={{0,4},{4,0},{8,12},{12,8},{1,5},{5,1},{9,13},{13,9},{2,6},{6,2},{1... | collective-permute-start | bytes 393224 | tf_op jit(solution)/shard_map/ppermute | solution.py:362
  32.8 2.8 %collective-permute-start.10 = (bf16[256,256]{1,0:T(8,128)(2,1)S(1)}, bf16[256,256]{1,0:T(8,128)(2,1)S(1)}, u32[]{:S(2)}, u32[]{:S(2)}) collective-permute-start(bf16[256,256]{1,0:T(8,128)(2,1)S(1)} %get-tuple-element.41.refs_3_.refs_5_), channel_id=1, source_target_pairs={{0,8},{4,12},{8,0},{12,4},{1,9},{5,13},{9,1},{13,5},{2,10},{6,14},... | collective-permute-start | bytes 393224 | tf_op jit(solution)/shard_map/ppermute | solution.py:363
  35.7 4.4 %shard_map.104 = (bf16[384,128]{1,0:T(8,128)(2,1)S(1)}, bf16[384,256]{1,0:T(8,128)(2,1)S(1)}) custom-call(s32[4]{0:T(128)S(1)} %pad_add_fusion.place_ref, s32[2]{0:T(128)S(1)} %copy-done.7, bf16[768,768]{1,0:T(8,128)(2,1)S(1)} %copy-done, bf16[768,768]{1,0:T(8,128)(2,1)} %collective-permute-done.refs_1_, bf16[384,768]{1,0:T(8,128)(2,1)} %collective-permute-done.8.refs_2_, ...), custom_call_target="tpu_custom_call" | custom-call | flops 384 | bytes 384 | tf_op jit(solution)/shard_map/pallas_call | solution.py:104
  40.1 1.6 %collective-permute-start.12 = (bf16[384,256]{1,0:T(8,128)(2,1)S(1)}, bf16[384,256]{1,0:T(8,128)(2,1)S(1)}, u32[]{:S(2)}, u32[]{:S(2)}) collective-permute-start(bf16[384,256]{1,0:T(8,128)(2,1)S(1)} %get-tuple-element.42.refs_3_), channel_id=1, source_target_pairs={{0,4},{4,0},{8,12},{12,8},{1,5},{5,1},{9,13},{13,9},{2,6},{6,2},{1... | collective-permute-start | bytes 589832 | tf_op jit(solution)/shard_map/ppermute | solution.py:362
  41.8 2.1 %collective-permute-start.11 = (bf16[384,256]{1,0:T(8,128)(2,1)S(1)}, bf16[384,256]{1,0:T(8,128)(2,1)S(1)}, u32[]{:S(2)}, u32[]{:S(2)}) collective-permute-start(bf16[384,256]{1,0:T(8,128)(2,1)S(1)} %get-tuple-element.42.refs_3_), channel_id=1, source_target_pairs={{0,8},{4,12},{8,0},{12,4},{1,9},{5,13},{9,1},{13,5},{2,10},{6,14},... | collective-permute-start | bytes 589832 | tf_op jit(solution)/shard_map/ppermute | solution.py:363
  43.9 2.5 %collective-permute-start.14 = (bf16[256,256]{1,0:T(8,128)(2,1)S(1)}, bf16[256,256]{1,0:T(8,128)(2,1)S(1)}, u32[]{:S(2)}, u32[]{:S(2)}) collective-permute-start(bf16[256,256]{1,0:T(8,128)(2,1)S(1)} %collective-permute-done.10.refs_10_), channel_id=1, source_target_pairs={{0,4},{4,0},{8,12},{12,8},{1,5},{5,1},{9,13},{13,9},{2,6},{6,2},{1... | collective-permute-start | bytes 393224 | tf_op jit(solution)/shard_map/ppermute | solution.py:362
  46.5 3.4 %shard_map.105 = (f32[768,128]{1,0:T(8,128)S(1)}, f32[768,128]{1,0:T(8,128)S(1)}, f32[768,128]{1,0:T(8,128)S(1)}) custom-call(s32[8]{0:T(128)S(1)} %pad_add_fusion.1.ids_ref, s32[2]{0:T(128)S(1)} %copy-done.7, s32[8,27]{1,0:T(8,128)S(1)} %copy-done.6, bf16[128,128]{1,0:T(8,128)(2,1)S(1)} %get-tuple-element.35.refs_0_, ...), custom_call_target="tpu_custom_call" | custom-call | flops 1327104 | bytes 98304 | tf_op jit(solution)/shard_map/pallas_call | solution.py:225
  49.9 3.7 %collective-permute-done.14.refs_3_ = bf16[256,256]{1,0:T(8,128)(2,1)S(1)} collective-permute-done((bf16[256,256]{1,0:T(8,128)(2,1)S(1)}, bf16[256,256]{1,0:T(8,128)(2,1)S(1)}, u32[]{:S(2)}, u32[]{:S(2)}) %collective-permute-start.14) | collective-permute-done | bytes 131104 | tf_op jit(solution)/shard_map/ppermute | solution.py:362
  53.6 1.6 %collective-permute-start.15 = (bf16[384,256]{1,0:T(8,128)(2,1)S(1)}, bf16[384,256]{1,0:T(8,128)(2,1)S(1)}, u32[]{:S(2)}, u32[]{:S(2)}) collective-permute-start(bf16[384,256]{1,0:T(8,128)(2,1)S(1)} %collective-permute-done.11.refs_5_), channel_id=1, source_target_pairs={{0,4},{4,0},{8,12},{12,8},{1,5},{5,1},{9,13},{13,9},{2,6},{6,2},{1... | collective-permute-start | bytes 589832 | tf_op jit(solution)/shard_map/ppermute | solution.py:362
  55.2 2.3 %shard_map.106 = (f32[768,128]{1,0:T(8,128)S(1)}, f32[768,128]{1,0:T(8,128)S(1)}, f32[768,128]{1,0:T(8,128)S(1)}) custom-call(s32[8]{0:T(128)S(1)} %pad_add_fusion.1.ids_ref, s32[2]{0:T(128)S(1)} %copy-done.7, s32[8,27]{1,0:T(8,128)S(1)} %copy-done.6, bf16[128,128]{1,0:T(8,128)(2,1)S(1)} %get-tuple-element.35.refs_0_, ...), custom_call_target="tpu_custom_call" | custom-call | flops 786432 | bytes 98304 | tf_op jit(solution)/shard_map/pallas_call | solution.py:225
  57.5 1.7 %collective-permute-done.15.refs_3_ = bf16[384,256]{1,0:T(8,128)(2,1)S(1)} collective-permute-done((bf16[384,256]{1,0:T(8,128)(2,1)S(1)}, bf16[384,256]{1,0:T(8,128)(2,1)S(1)}, u32[]{:S(2)}, u32[]{:S(2)}) %collective-permute-start.15) | collective-permute-done | bytes 196640 | tf_op jit(solution)/shard_map/ppermute | solution.py:362
  59.3 1.7 %shard_map.107.refs_0_ = bf16[768,128]{1,0:T(8,128)(2,1)S(1)} custom-call(s32[8]{0:T(128)S(1)} %pad_add_fusion.1.ids_ref, s32[2]{0:T(128)S(1)} %copy-done.7, s32[8,27]{1,0:T(8,128)S(1)} %copy-done.6, bf16[128,128]{1,0:T(8,128)(2,1)S(1)} %get-tuple-element.35.refs_0_, bf16[256,128]{1,0:T(8,128)(2,1)S(1)} %get-tuple-element.36.refs_1_, ...), custom_call_target="tpu_custom_call" | custom-call | flops 294912 | bytes 98304 | tf_op jit(solution)/shard_map/pallas_call | solution.py:225
  62.6 4.2 %collective-permute-done.17.refs_2_ = bf16[768,128]{1,0:T(8,128)(2,1)S(1)} collective-permute-done((bf16[768,128]{1,0:T(8,128)(2,1)S(1)}, bf16[768,128]{1,0:T(8,128)(2,1)S(1)}, u32[]{:S(2)}, u32[]{:S(2)}) %collective-permute-start.17) | collective-permute-done | bytes 196640 | tf_op jit(solution)/shard_map/ppermute | solution.py:287
  68.2 2.2 %shard_map.108 = bf16[768,768]{1,0:T(8,128)(2,1)} custom-call(s32[4]{0:T(128)S(1)} %pad_add_fusion.place_ref, bf16[768,128]{1,0:T(8,128)(2,1)S(1)} %shard_map.107.refs_0_, bf16[768,128]{1,0:T(8,128)(2,1)S(1)} %collective-permute-done.16.refs_1_, bf16[768,128]{1,0:T(8,128)(2,1)S(1)} %collective-permute-done.17.refs_2_, ...), custom_call_target="tpu_custom_call" | custom-call | flops 603979776 | bytes 3932160 | tf_op jit(solution)/shard_map/pallas_call | solution.py:267
  (51 shorter events, 9.1 us)
Async XLA Ops:
  0.0 11.8 %collective-permute-start = (bf16[768,768]{1,0:T(8,128)(2,1)}, bf16[768,768]{1,0:T(8,128)(2,1)}, u32[]{:S(2)}, u32[]{:S(2)}) collective-permute-start(bf16[768,768]{1,0:T(8,128)(2,1)} %refs_5_.3), channel_id=1, source_target_pairs={{0,1},{1,0},{2,3},{3,2},{4,5},{5,4},{6,7},{7,6},{8,9},{9,8},{10,11... | collective-permute-start | bytes 3538952 | tf_op jit(solution)/shard_map/ppermute | solution.py:287
  1.4 8.4 %collective-permute-start.1 = (bf16[128,768]{1,0:T(8,128)(2,1)S(1)}, bf16[128,768]{1,0:T(8,128)(2,1)}, u32[]{:S(2)}, u32[]{:S(2)}) collective-permute-start(bf16[128,768]{1,0:T(8,128)(2,1)S(1)} %slice.18), channel_id=1, source_target_pairs={{0,2},{2,0},{1,3},{3,1},{4,6},{6,4},{5,7},{7,5},{8,10},{10,8},{9,1... | collective-permute-start | bytes 589832 | tf_op jit(solution)/shard_map/ppermute | solution.py:287
  5.7 12.5 %collective-permute-start.5 = (bf16[256,768]{1,0:T(8,128)(2,1)}, bf16[256,768]{1,0:T(8,128)(2,1)}, u32[]{:S(2)}, u32[]{:S(2)}) collective-permute-start(bf16[256,768]{1,0:T(8,128)(2,1)} %slice.22), channel_id=1, source_target_pairs={{0,2},{2,0},{1,3},{3,1},{4,6},{6,4},{5,7},{7,5},{8,10},{10,8},{9,1... | collective-permute-start | bytes 1179656 | tf_op jit(solution)/shard_map/ppermute | solution.py:287
  9.3 2.5 %copy-start.9 = (f32[128]{0:T(128)S(1)}, f32[128]{0:T(128)}, u32[]{:S(2)}) copy-start(f32[128]{0:T(128)} %param.14) | copy-start | bytes 1540
  9.8 2.0 %collective-permute-start.2 = (bf16[128,768]{1,0:T(8,128)(2,1)}, bf16[128,768]{1,0:T(8,128)(2,1)}, u32[]{:S(2)}, u32[]{:S(2)}) collective-permute-start(bf16[128,768]{1,0:T(8,128)(2,1)} %collective-permute-done.1.refs_2_), channel_id=1, source_target_pairs={{0,1},{1,0},{2,3},{3,2},{4,5},{5,4},{6,7},{7,6},{8,9},{9,8},{10,11... | collective-permute-start | bytes 589832 | tf_op jit(solution)/shard_map/ppermute | solution.py:287
  9.8 20.9 %collective-permute-start.8 = (bf16[384,768]{1,0:T(8,128)(2,1)}, bf16[384,768]{1,0:T(8,128)(2,1)}, u32[]{:S(2)}, u32[]{:S(2)}) collective-permute-start(bf16[384,768]{1,0:T(8,128)(2,1)} %slice.19), channel_id=1, source_target_pairs={{0,2},{2,0},{1,3},{3,1},{4,6},{6,4},{5,7},{7,5},{8,10},{10,8},{9,1... | collective-permute-start | bytes 1769480 | tf_op jit(solution)/shard_map/ppermute | solution.py:287
  12.7 10.9 %copy-start.3 = (f32[3,3072]{1,0:T(4,128)S(1)}, f32[3,3072]{1,0:T(4,128)}, u32[]{:S(2)}) copy-start(f32[3,3072]{1,0:T(4,128)} %refs_6_.1) | copy-start | bytes 110596
  18.2 5.3 %collective-permute-start.6 = (bf16[256,768]{1,0:T(8,128)(2,1)}, bf16[256,768]{1,0:T(8,128)(2,1)S(1)}, u32[]{:S(2)}, u32[]{:S(2)}) collective-permute-start(bf16[256,768]{1,0:T(8,128)(2,1)} %collective-permute-done.5.refs_2_), channel_id=1, source_target_pairs={{0,1},{1,0},{2,3},{3,2},{4,5},{5,4},{6,7},{7,6},{8,9},{9,8},{10,11... | collective-permute-start | bytes 1179656 | tf_op jit(solution)/shard_map/ppermute | solution.py:287
  18.2 12.5 %collective-permute-start.4 = (bf16[144,256]{1,0:T(8,128)(2,1)S(1)}, bf16[144,256]{1,0:T(8,128)(2,1)S(1)}, u32[]{:S(2)}, u32[]{:S(2)}) collective-permute-start(bf16[144,256]{1,0:T(8,128)(2,1)S(1)} %get-tuple-element.31.refs_2_.refs_4_), channel_id=1, source_target_pairs={{0,8},{4,12},{8,0},{12,4},{1,9},{5,13},{9,1},{13,5},{2,10},{6,14},... | collective-permute-start | bytes 221192 | tf_op jit(solution)/shard_map/ppermute | solution.py:363
  21.3 9.4 %collective-permute-start.3 = (bf16[144,256]{1,0:T(8,128)(2,1)S(1)}, bf16[144,256]{1,0:T(8,128)(2,1)S(1)}, u32[]{:S(2)}, u32[]{:S(2)}) collective-permute-start(bf16[144,256]{1,0:T(8,128)(2,1)S(1)} %get-tuple-element.31.refs_2_.refs_4_), channel_id=1, source_target_pairs={{0,4},{4,0},{8,12},{12,8},{1,5},{5,1},{9,13},{13,9},{2,6},{6,2},{1... | collective-permute-start | bytes 221192 | tf_op jit(solution)/shard_map/ppermute | solution.py:362
  23.5 3.8 %copy-start.5 = (bf16[256,256]{1,0:T(8,128)(2,1)S(1)}, bf16[256,256]{1,0:T(8,128)(2,1)}, u32[]{:S(2)}) copy-start(bf16[256,256]{1,0:T(8,128)(2,1)} %refs_12_.1) | copy-start | bytes 393220
  23.5 3.8 %copy-start.6 = (s32[8,27]{1,0:T(8,128)S(1)}, s32[8,27]{1,0:T(8,128)}, u32[]{:S(2)}) copy-start(s32[8,27]{1,0:T(8,128)} %windows_ref.7) | copy-start | bytes 2596
  30.7 5.0 %collective-permute-start.9 = (bf16[384,768]{1,0:T(8,128)(2,1)}, bf16[384,768]{1,0:T(8,128)(2,1)S(1)}, u32[]{:S(2)}, u32[]{:S(2)}) collective-permute-start(bf16[384,768]{1,0:T(8,128)(2,1)} %collective-permute-done.8.refs_2_), channel_id=1, source_target_pairs={{0,1},{1,0},{2,3},{3,2},{4,5},{5,4},{6,7},{7,6},{8,9},{9,8},{10,11... | collective-permute-start | bytes 1769480 | tf_op jit(solution)/shard_map/ppermute | solution.py:287
  30.7 13.1 %collective-permute-start.13 = (bf16[256,256]{1,0:T(8,128)(2,1)S(1)}, bf16[256,256]{1,0:T(8,128)(2,1)S(1)}, u32[]{:S(2)}, u32[]{:S(2)}) collective-permute-start(bf16[256,256]{1,0:T(8,128)(2,1)S(1)} %get-tuple-element.41.refs_3_.refs_5_), channel_id=1, source_target_pairs={{0,4},{4,0},{8,12},{12,8},{1,5},{5,1},{9,13},{13,9},{2,6},{6,2},{1... | collective-permute-start | bytes 393224 | tf_op jit(solution)/shard_map/ppermute | solution.py:362
  32.6 11.2 %collective-permute-start.7 = (bf16[144,256]{1,0:T(8,128)(2,1)S(1)}, bf16[144,256]{1,0:T(8,128)(2,1)S(1)}, u32[]{:S(2)}, u32[]{:S(2)}) collective-permute-start(bf16[144,256]{1,0:T(8,128)(2,1)S(1)} %collective-permute-done.4.refs_7_), channel_id=1, source_target_pairs={{0,4},{4,0},{8,12},{12,8},{1,5},{5,1},{9,13},{13,9},{2,6},{6,2},{1... | collective-permute-start | bytes 221192 | tf_op jit(solution)/shard_map/ppermute | solution.py:362
  32.8 8.9 %collective-permute-start.10 = (bf16[256,256]{1,0:T(8,128)(2,1)S(1)}, bf16[256,256]{1,0:T(8,128)(2,1)S(1)}, u32[]{:S(2)}, u32[]{:S(2)}) collective-permute-start(bf16[256,256]{1,0:T(8,128)(2,1)S(1)} %get-tuple-element.41.refs_3_.refs_5_), channel_id=1, source_target_pairs={{0,8},{4,12},{8,0},{12,4},{1,9},{5,13},{9,1},{13,5},{2,10},{6,14},... | collective-permute-start | bytes 393224 | tf_op jit(solution)/shard_map/ppermute | solution.py:363
  40.1 13.5 %collective-permute-start.12 = (bf16[384,256]{1,0:T(8,128)(2,1)S(1)}, bf16[384,256]{1,0:T(8,128)(2,1)S(1)}, u32[]{:S(2)}, u32[]{:S(2)}) collective-permute-start(bf16[384,256]{1,0:T(8,128)(2,1)S(1)} %get-tuple-element.42.refs_3_), channel_id=1, source_target_pairs={{0,4},{4,0},{8,12},{12,8},{1,5},{5,1},{9,13},{13,9},{2,6},{6,2},{1... | collective-permute-start | bytes 589832 | tf_op jit(solution)/shard_map/ppermute | solution.py:362
  41.8 11.9 %collective-permute-start.11 = (bf16[384,256]{1,0:T(8,128)(2,1)S(1)}, bf16[384,256]{1,0:T(8,128)(2,1)S(1)}, u32[]{:S(2)}, u32[]{:S(2)}) collective-permute-start(bf16[384,256]{1,0:T(8,128)(2,1)S(1)} %get-tuple-element.42.refs_3_), channel_id=1, source_target_pairs={{0,8},{4,12},{8,0},{12,4},{1,9},{5,13},{9,1},{13,5},{2,10},{6,14},... | collective-permute-start | bytes 589832 | tf_op jit(solution)/shard_map/ppermute | solution.py:363
  43.9 9.7 %collective-permute-start.14 = (bf16[256,256]{1,0:T(8,128)(2,1)S(1)}, bf16[256,256]{1,0:T(8,128)(2,1)S(1)}, u32[]{:S(2)}, u32[]{:S(2)}) collective-permute-start(bf16[256,256]{1,0:T(8,128)(2,1)S(1)} %collective-permute-done.10.refs_10_), channel_id=1, source_target_pairs={{0,4},{4,0},{8,12},{12,8},{1,5},{5,1},{9,13},{13,9},{2,6},{6,2},{1... | collective-permute-start | bytes 393224 | tf_op jit(solution)/shard_map/ppermute | solution.py:362
  53.6 5.7 %collective-permute-start.15 = (bf16[384,256]{1,0:T(8,128)(2,1)S(1)}, bf16[384,256]{1,0:T(8,128)(2,1)S(1)}, u32[]{:S(2)}, u32[]{:S(2)}) collective-permute-start(bf16[384,256]{1,0:T(8,128)(2,1)S(1)} %collective-permute-done.11.refs_5_), channel_id=1, source_target_pairs={{0,4},{4,0},{8,12},{12,8},{1,5},{5,1},{9,13},{13,9},{2,6},{6,2},{1... | collective-permute-start | bytes 589832 | tf_op jit(solution)/shard_map/ppermute | solution.py:362
  57.5 10.6 %copy-start.4 = (bf16[512,768]{1,0:T(8,128)(2,1)S(1)}, bf16[512,768]{1,0:T(8,128)(2,1)}, u32[]{:S(2)}) copy-start(bf16[512,768]{1,0:T(8,128)(2,1)} %refs_4_.8) | copy-start | bytes 2359300
  61.0 5.7 %collective-permute-start.17 = (bf16[768,128]{1,0:T(8,128)(2,1)S(1)}, bf16[768,128]{1,0:T(8,128)(2,1)S(1)}, u32[]{:S(2)}, u32[]{:S(2)}) collective-permute-start(bf16[768,128]{1,0:T(8,128)(2,1)S(1)} %shard_map.107.refs_0_), channel_id=1, source_target_pairs={{0,2},{2,0},{1,3},{3,1},{4,6},{6,4},{5,7},{7,5},{8,10},{10,8},{9,1... | collective-permute-start | bytes 589832 | tf_op jit(solution)/shard_map/ppermute | solution.py:287
  62.6 4.2 %collective-permute-start.16 = (bf16[768,128]{1,0:T(8,128)(2,1)S(1)}, bf16[768,128]{1,0:T(8,128)(2,1)S(1)}, u32[]{:S(2)}, u32[]{:S(2)}) collective-permute-start(bf16[768,128]{1,0:T(8,128)(2,1)S(1)} %shard_map.107.refs_0_), channel_id=1, source_target_pairs={{0,1},{1,0},{2,3},{3,2},{4,5},{5,4},{6,7},{7,6},{8,9},{9,8},{10,11... | collective-permute-start | bytes 589832 | tf_op jit(solution)/shard_map/ppermute | solution.py:287
  66.7 1.4 %collective-permute-start.18 = (bf16[768,128]{1,0:T(8,128)(2,1)S(1)}, bf16[768,128]{1,0:T(8,128)(2,1)S(1)}, u32[]{:S(2)}, u32[]{:S(2)}) collective-permute-start(bf16[768,128]{1,0:T(8,128)(2,1)S(1)} %collective-permute-done.17.refs_2_), channel_id=1, source_target_pairs={{0,1},{1,0},{2,3},{3,2},{4,5},{5,4},{6,7},{7,6},{8,9},{9,8},{10,11... | collective-permute-start | bytes 589832 | tf_op jit(solution)/shard_map/ppermute | solution.py:287
  (5 other events, 10.0 us)

commit v2 on v1

--- a/solution.py
+++ b/solution.py
@@ -36,34 +36,29 @@
     sources = refs[:count]
     refs = refs[:count] + refs[count + after :]
     modulation_ref, query_gain_ref, key_gain_ref, weight_ref = refs[count : count + 4]
-    query_ref, kv_ref, pieces_ref, piece_sem = refs[count + 4 :]
+    query_ref, kv_ref = refs[count + 4 :]
     width = sources[0].shape[1]
     features = width * count
     spans = []
-    piece_copies = []
+    pieces = []
     for place, (source, start) in enumerate(zip(sources, starts)):
         first = place_ref[place] * width
         if count > 1:
             first = pl.multiple_of(first, width)
         spans.append(pl.ds(first, width))
-        piece_copies.append(
-            pltpu.make_async_copy(source.at[start : start + rows, :], pieces_ref.at[place], piece_sem.at[place])
-        )
-    for copy in piece_copies:
-        copy.start()
+        pieces.append(source.at[start : start + rows, :])
     total = 0.0
-    for place, copy in enumerate(piece_copies):
-        copy.wait()
-        total = total + jnp.sum(pieces_ref[place].astype(jnp.float32), axis=1, keepdims=True)
+    for piece in pieces:
+        total = total + jnp.sum(piece[...].astype(jnp.float32), axis=1, keepdims=True)
     average = total / features
     spread = 0.0
     for place in range(count):
-        centred = pieces_ref[place].astype(jnp.float32) - average
+        centred = pieces[place][...].astype(jnp.float32) - average
         spread = spread + jnp.sum(centred * centred, axis=1, keepdims=True)
     scale = lax.rsqrt(spread / features + epsilon)
     projected = 0.0
     for place, span in enumerate(spans):
-        centred = pieces_ref[place].astype(jnp.float32) - average
+        centred = pieces[place][...].astype(jnp.float32) - average
         modulated = (
             centred * scale * (1.0 + modulation_ref[1:2, span]) + modulation_ref[0:1, span]
         ).astype(jnp.bfloat16)
@@ -107,12 +102,8 @@
             jax.ShapeDtypeStruct((rows, HD), jnp.bfloat16),
             jax.ShapeDtypeStruct((rows + labels, 2 * HD), jnp.bfloat16),
         ),
-        in_specs=[SMEM] * 2 + [HBM] * count + [ANY] * len(after) + [VMEM] * 4,
+        in_specs=[SMEM] * 2 + [VMEM] * count + [ANY] * len(after) + [VMEM] * 4,
         out_specs=(VMEM, VMEM),
-        scratch_shapes=[
-            pltpu.VMEM((count, rows, width), jnp.bfloat16),
-            pltpu.SemaphoreType.DMA((count,)),
-        ],
         compiler_params=pltpu.CompilerParams(vmem_limit_bytes=PROJECT_LIMIT),
         cost_estimate=pl.CostEstimate(flops=rows, bytes_accessed=rows, transcendentals=rows),
     )(places, ids, *pieces, *after, modulation, query_gain, key_gain, weight)

time: 70.6 us -> 70 us (level)
  waiting for transfers between devices: 15.9 us -> 14.6 us
    ppermute x6, waiting for transfers between devices: 5.46 us -> 3.16 us  [body(): near = lambda values: lax.ppermute(values, 'tiles', NEAR)]
    pallas_call x4, Pallas kernels: 8.81 us -> 10.7 us  [attend(): pl.pallas_call(functools.partial(attend_kernel, [at for at, array in quer...]
    pallas_call x3, Pallas kernels: 11.1 us -> 9.7 us  [project(): pl.pallas_call(functools.partial(project_kernel, count, len(after), start...]
    ppermute x10, waiting for transfers between devices: 10.5 us -> 11.5 us  [shifted(): lax.ppermute(values, axis, [(at, (at + by) % size) for at in range(size)])]
  transfers between devices with their start and end apart: 19 -> 19, of which waited for: 7 -> 7; matrix products, arithmetic and copies ran while one was open for 7% -> 7% of each run, Pallas kernels for 26% -> 27%
where the time goes in v2:
time: 70 us
  starting transfers between devices  24.4 us (35%)
  Pallas kernels  22.8 us (33%)
  waiting for transfers between devices  14.6 us (21%)
  local copies, waits for them, and re-layouts  7.12 us (10%)
  between operations  0.84 us (1%)
    ppermute x10, waiting for transfers between devices, shifted(): lax.ppermute(values, axis, [(at, (at + by) % size) for at in range(size)])  11.5 us
    pallas_call x4, Pallas kernels, attend(): pl.pallas_call(functools.partial(attend_kernel, [at for at, array in quer...  10.7 us
    pallas_call x3, Pallas kernels, project(): pl.pallas_call(functools.partial(project_kernel, count, len(after), start...  9.7 us
    ppermute x6, starting transfers between devices, body(): near = lambda values: lax.ppermute(values, 'tiles', NEAR)  9.46 us
    ppermute x3, starting transfers between devices, body(): away = lambda values: lax.ppermute(values, 'tiles', AWAY)  8.43 us
    ppermute x10, starting transfers between devices, shifted(): lax.ppermute(values, axis, [(at, (at + by) % size) for at in range(size)])  6.53 us
    slice x2, local copies, waits for them, and re-layouts, body(): parts += [rest[start:start + size] for start, size in CHUNKS[1:]]  3.68 us
    ppermute x6, waiting for transfers between devices, body(): near = lambda values: lax.ppermute(values, 'tiles', NEAR)  3.16 us
  transfers between devices with their start and end apart: 19, of which 7 were waited for; matrix products, arithmetic and copies ran while one was open for 7% of the time, Pallas kernels for 27%

profile of v2, /device:TPU:0, one launch (start us, length us, event | category | flops | bytes accessed | tf_op | source)
XLA Modules:
  0.0 70.0 jit_solution(216073299105764491)
XLA Ops:
  1.4 2.6 %collective-permute-start.1 = (bf16[128,768]{1,0:T(8,128)(2,1)S(1)}, bf16[128,768]{1,0:T(8,128)(2,1)}, u32[]{:S(2)}, u32[]{:S(2)}) collective-permute-start(bf16[128,768]{1,0:T(8,128)(2,1)S(1)} %slice.18), channel_id=1, source_target_pairs={{0,2},{2,0},{1,3},{3,1},{4,6},{6,4},{5,7},{7,5},{8,10},{10,8},{9,1... | collective-permute-start | bytes 589832 | tf_op jit(solution)/shard_map/ppermute | solution.py:278
  4.0 1.8 %slice.22 = bf16[256,768]{1,0:T(8,128)(2,1)} slice(bf16[768,768]{1,0:T(8,128)(2,1)} %refs_5_.3), slice={[128:384], [0:768]} | slice | bytes 786432 | tf_op jit(solution)/shard_map/slice | solution.py:321
  5.7 1.9 %slice.19 = bf16[384,768]{1,0:T(8,128)(2,1)} slice(bf16[768,768]{1,0:T(8,128)(2,1)} %refs_5_.3), slice={[384:768], [0:768]} | slice | bytes 1179648 | tf_op jit(solution)/shard_map/slice | solution.py:321
  7.7 1.7 %copy-done.1 = bf16[3072,384]{1,0:T(8,128)(2,1)S(1)} copy-done((bf16[3072,384]{1,0:T(8,128)(2,1)S(1)}, bf16[3072,384]{1,0:T(8,128)(2,1)}, u32[]{:S(2)}) %copy-start.1) | copy-done | bytes 2359320
  9.8 1.9 %collective-permute-start.8 = (bf16[384,768]{1,0:T(8,128)(2,1)}, bf16[384,768]{1,0:T(8,128)(2,1)}, u32[]{:S(2)}, u32[]{:S(2)}) collective-permute-start(bf16[384,768]{1,0:T(8,128)(2,1)} %slice.19), channel_id=1, source_target_pairs={{0,2},{2,0},{1,3},{3,1},{4,6},{6,4},{5,7},{7,5},{8,10},{10,8},{9,1... | collective-permute-start | bytes 1769480 | tf_op jit(solution)/shard_map/ppermute | solution.py:278
  12.7 2.5 %shard_map.101 = (bf16[128,128]{1,0:T(8,128)(2,1)S(1)}, bf16[144,256]{1,0:T(8,128)(2,1)S(1)}) custom-call(s32[4]{0:T(128)S(1)} %pad_add_fusion.place_ref, s32[2]{0:T(128)S(1)} %copy-done.7, bf16[768,768]{1,0:T(8,128)(2,1)S(1)} %copy-done, bf16[768,768]{1,0:T(8,128)(2,1)} %collective-permute-done.refs_1_, bf16[128,768]{1,0:T(8,128)(2,1)} %collective-permute-done.1.refs_2_, ...), custom_call_target="tpu_custom_call" | custom-call | flops 128 | bytes 128 | tf_op jit(solution)/shard_map/pallas_call | solution.py:99
  15.2 3.1 %collective-permute-done.5.refs_2_ = bf16[256,768]{1,0:T(8,128)(2,1)} collective-permute-done((bf16[256,768]{1,0:T(8,128)(2,1)}, bf16[256,768]{1,0:T(8,128)(2,1)}, u32[]{:S(2)}, u32[]{:S(2)}) %collective-permute-start.5) | collective-permute-done | bytes 393248 | tf_op jit(solution)/shard_map/ppermute | solution.py:278
  18.2 3.0 %collective-permute-start.4 = (bf16[144,256]{1,0:T(8,128)(2,1)S(1)}, bf16[144,256]{1,0:T(8,128)(2,1)S(1)}, u32[]{:S(2)}, u32[]{:S(2)}) collective-permute-start(bf16[144,256]{1,0:T(8,128)(2,1)S(1)} %get-tuple-element.31.refs_2_.refs_4_), channel_id=1, source_target_pairs={{0,8},{4,12},{8,0},{12,4},{1,9},{5,13},{9,1},{13,5},{2,10},{6,14},... | collective-permute-start | bytes 221192 | tf_op jit(solution)/shard_map/ppermute | solution.py:354
  21.3 1.6 %collective-permute-start.3 = (bf16[144,256]{1,0:T(8,128)(2,1)S(1)}, bf16[144,256]{1,0:T(8,128)(2,1)S(1)}, u32[]{:S(2)}, u32[]{:S(2)}) collective-permute-start(bf16[144,256]{1,0:T(8,128)(2,1)S(1)} %get-tuple-element.31.refs_2_.refs_4_), channel_id=1, source_target_pairs={{0,4},{4,0},{8,12},{12,8},{1,5},{5,1},{9,13},{13,9},{2,6},{6,2},{1... | collective-permute-start | bytes 221192 | tf_op jit(solution)/shard_map/ppermute | solution.py:353
  23.6 3.2 %shard_map.102 = (bf16[256,128]{1,0:T(8,128)(2,1)S(1)}, bf16[256,256]{1,0:T(8,128)(2,1)S(1)}) custom-call(s32[4]{0:T(128)S(1)} %pad_add_fusion.place_ref, s32[2]{0:T(128)S(1)} %copy-done.7, bf16[768,768]{1,0:T(8,128)(2,1)S(1)} %copy-done, bf16[768,768]{1,0:T(8,128)(2,1)} %collective-permute-done.refs_1_, bf16[256,768]{1,0:T(8,128)(2,1)} %collective-permute-done.5.refs_2_, ...), custom_call_target="tpu_custom_call" | custom-call | flops 256 | bytes 256 | tf_op jit(solution)/shard_map/pallas_call | solution.py:99
  28.2 2.5 %collective-permute-done.8.refs_2_ = bf16[384,768]{1,0:T(8,128)(2,1)} collective-permute-done((bf16[384,768]{1,0:T(8,128)(2,1)}, bf16[384,768]{1,0:T(8,128)(2,1)}, u32[]{:S(2)}, u32[]{:S(2)}) %collective-permute-start.8) | collective-permute-done | bytes 589856 | tf_op jit(solution)/shard_map/ppermute | solution.py:278
  30.7 1.9 %collective-permute-start.13 = (bf16[256,256]{1,0:T(8,128)(2,1)S(1)}, bf16[256,256]{1,0:T(8,128)(2,1)S(1)}, u32[]{:S(2)}, u32[]{:S(2)}) collective-permute-start(bf16[256,256]{1,0:T(8,128)(2,1)S(1)} %get-tuple-element.41.refs_3_.refs_5_), channel_id=1, source_target_pairs={{0,4},{4,0},{8,12},{12,8},{1,5},{5,1},{9,13},{13,9},{2,6},{6,2},{1... | collective-permute-start | bytes 393224 | tf_op jit(solution)/shard_map/ppermute | solution.py:353
  32.8 2.8 %collective-permute-start.10 = (bf16[256,256]{1,0:T(8,128)(2,1)S(1)}, bf16[256,256]{1,0:T(8,128)(2,1)S(1)}, u32[]{:S(2)}, u32[]{:S(2)}) collective-permute-start(bf16[256,256]{1,0:T(8,128)(2,1)S(1)} %get-tuple-element.41.refs_3_.refs_5_), channel_id=1, source_target_pairs={{0,8},{4,12},{8,0},{12,4},{1,9},{5,13},{9,1},{13,5},{2,10},{6,14},... | collective-permute-start | bytes 393224 | tf_op jit(solution)/shard_map/ppermute | solution.py:354
  35.7 4.0 %shard_map.104 = (bf16[384,128]{1,0:T(8,128)(2,1)S(1)}, bf16[384,256]{1,0:T(8,128)(2,1)S(1)}) custom-call(s32[4]{0:T(128)S(1)} %pad_add_fusion.place_ref, s32[2]{0:T(128)S(1)} %copy-done.7, bf16[768,768]{1,0:T(8,128)(2,1)S(1)} %copy-done, bf16[768,768]{1,0:T(8,128)(2,1)} %collective-permute-done.refs_1_, bf16[384,768]{1,0:T(8,128)(2,1)} %collective-permute-done.8.refs_2_, ...), custom_call_target="tpu_custom_call" | custom-call | flops 384 | bytes 384 | tf_op jit(solution)/shard_map/pallas_call | solution.py:99
  39.7 1.6 %collective-permute-start.12 = (bf16[384,256]{1,0:T(8,128)(2,1)S(1)}, bf16[384,256]{1,0:T(8,128)(2,1)S(1)}, u32[]{:S(2)}, u32[]{:S(2)}) collective-permute-start(bf16[384,256]{1,0:T(8,128)(2,1)S(1)} %get-tuple-element.42.refs_3_), channel_id=1, source_target_pairs={{0,4},{4,0},{8,12},{12,8},{1,5},{5,1},{9,13},{13,9},{2,6},{6,2},{1... | collective-permute-start | bytes 589832 | tf_op jit(solution)/shard_map/ppermute | solution.py:353
  41.3 2.6 %collective-permute-start.11 = (bf16[384,256]{1,0:T(8,128)(2,1)S(1)}, bf16[384,256]{1,0:T(8,128)(2,1)S(1)}, u32[]{:S(2)}, u32[]{:S(2)}) collective-permute-start(bf16[384,256]{1,0:T(8,128)(2,1)S(1)} %get-tuple-element.42.refs_3_), channel_id=1, source_target_pairs={{0,8},{4,12},{8,0},{12,4},{1,9},{5,13},{9,1},{13,5},{2,10},{6,14},... | collective-permute-start | bytes 589832 | tf_op jit(solution)/shard_map/ppermute | solution.py:354
  43.9 2.5 %collective-permute-start.14 = (bf16[256,256]{1,0:T(8,128)(2,1)S(1)}, bf16[256,256]{1,0:T(8,128)(2,1)S(1)}, u32[]{:S(2)}, u32[]{:S(2)}) collective-permute-start(bf16[256,256]{1,0:T(8,128)(2,1)S(1)} %collective-permute-done.10.refs_10_), channel_id=1, source_target_pairs={{0,4},{4,0},{8,12},{12,8},{1,5},{5,1},{9,13},{13,9},{2,6},{6,2},{1... | collective-permute-start | bytes 393224 | tf_op jit(solution)/shard_map/ppermute | solution.py:353
  46.5 4.5 %shard_map.105 = (f32[768,128]{1,0:T(8,128)S(1)}, f32[768,128]{1,0:T(8,128)S(1)}, f32[768,128]{1,0:T(8,128)S(1)}) custom-call(s32[8]{0:T(128)S(1)} %pad_add_fusion.1.ids_ref, s32[2]{0:T(128)S(1)} %copy-done.7, s32[8,27]{1,0:T(8,128)S(1)} %copy-done.6, bf16[128,128]{1,0:T(8,128)(2,1)S(1)} %get-tuple-element.35.refs_0_, ...), custom_call_target="tpu_custom_call" | custom-call | flops 1327104 | bytes 98304 | tf_op jit(solution)/shard_map/pallas_call | solution.py:216
  51.0 2.2 %collective-permute-done.14.refs_3_ = bf16[256,256]{1,0:T(8,128)(2,1)S(1)} collective-permute-done((bf16[256,256]{1,0:T(8,128)(2,1)S(1)}, bf16[256,256]{1,0:T(8,128)(2,1)S(1)}, u32[]{:S(2)}, u32[]{:S(2)}) %collective-permute-start.14) | collective-permute-done | bytes 131104 | tf_op jit(solution)/shard_map/ppermute | solution.py:353
  53.2 1.6 %collective-permute-start.15 = (bf16[384,256]{1,0:T(8,128)(2,1)S(1)}, bf16[384,256]{1,0:T(8,128)(2,1)S(1)}, u32[]{:S(2)}, u32[]{:S(2)}) collective-permute-start(bf16[384,256]{1,0:T(8,128)(2,1)S(1)} %collective-permute-done.11.refs_5_), channel_id=1, source_target_pairs={{0,4},{4,0},{8,12},{12,8},{1,5},{5,1},{9,13},{13,9},{2,6},{6,2},{1... | collective-permute-start | bytes 589832 | tf_op jit(solution)/shard_map/ppermute | solution.py:353
  54.8 3.1 %shard_map.106 = (f32[768,128]{1,0:T(8,128)S(1)}, f32[768,128]{1,0:T(8,128)S(1)}, f32[768,128]{1,0:T(8,128)S(1)}) custom-call(s32[8]{0:T(128)S(1)} %pad_add_fusion.1.ids_ref, s32[2]{0:T(128)S(1)} %copy-done.7, s32[8,27]{1,0:T(8,128)S(1)} %copy-done.6, bf16[128,128]{1,0:T(8,128)(2,1)S(1)} %get-tuple-element.35.refs_0_, ...), custom_call_target="tpu_custom_call" | custom-call | flops 786432 | bytes 98304 | tf_op jit(solution)/shard_map/pallas_call | solution.py:216
  58.8 1.7 %shard_map.107.refs_0_ = bf16[768,128]{1,0:T(8,128)(2,1)S(1)} custom-call(s32[8]{0:T(128)S(1)} %pad_add_fusion.1.ids_ref, s32[2]{0:T(128)S(1)} %copy-done.7, s32[8,27]{1,0:T(8,128)S(1)} %copy-done.6, bf16[128,128]{1,0:T(8,128)(2,1)S(1)} %get-tuple-element.35.refs_0_, bf16[256,128]{1,0:T(8,128)(2,1)S(1)} %get-tuple-element.36.refs_1_, ...), custom_call_target="tpu_custom_call" | custom-call | flops 294912 | bytes 98304 | tf_op jit(solution)/shard_map/pallas_call | solution.py:216
  62.1 4.2 %collective-permute-done.17.refs_2_ = bf16[768,128]{1,0:T(8,128)(2,1)S(1)} collective-permute-done((bf16[768,128]{1,0:T(8,128)(2,1)S(1)}, bf16[768,128]{1,0:T(8,128)(2,1)S(1)}, u32[]{:S(2)}, u32[]{:S(2)}) %collective-permute-start.17) | collective-permute-done | bytes 196640 | tf_op jit(solution)/shard_map/ppermute | solution.py:278
  67.7 2.2 %shard_map.108 = bf16[768,768]{1,0:T(8,128)(2,1)} custom-call(s32[4]{0:T(128)S(1)} %pad_add_fusion.place_ref, bf16[768,128]{1,0:T(8,128)(2,1)S(1)} %shard_map.107.refs_0_, bf16[768,128]{1,0:T(8,128)(2,1)S(1)} %collective-permute-done.16.refs_1_, bf16[768,128]{1,0:T(8,128)(2,1)S(1)} %collective-permute-done.17.refs_2_, ...), custom_call_target="tpu_custom_call" | custom-call | flops 603979776 | bytes 3932160 | tf_op jit(solution)/shard_map/pallas_call | solution.py:258
  (51 shorter events, 8.5 us)
Async XLA Ops:
  0.0 11.8 %collective-permute-start = (bf16[768,768]{1,0:T(8,128)(2,1)}, bf16[768,768]{1,0:T(8,128)(2,1)}, u32[]{:S(2)}, u32[]{:S(2)}) collective-permute-start(bf16[768,768]{1,0:T(8,128)(2,1)} %refs_5_.3), channel_id=1, source_target_pairs={{0,1},{1,0},{2,3},{3,2},{4,5},{5,4},{6,7},{7,6},{8,9},{9,8},{10,11... | collective-permute-start | bytes 3538952 | tf_op jit(solution)/shard_map/ppermute | solution.py:278
  1.4 8.4 %collective-permute-start.1 = (bf16[128,768]{1,0:T(8,128)(2,1)S(1)}, bf16[128,768]{1,0:T(8,128)(2,1)}, u32[]{:S(2)}, u32[]{:S(2)}) collective-permute-start(bf16[128,768]{1,0:T(8,128)(2,1)S(1)} %slice.18), channel_id=1, source_target_pairs={{0,2},{2,0},{1,3},{3,1},{4,6},{6,4},{5,7},{7,5},{8,10},{10,8},{9,1... | collective-permute-start | bytes 589832 | tf_op jit(solution)/shard_map/ppermute | solution.py:278
  5.7 12.5 %collective-permute-start.5 = (bf16[256,768]{1,0:T(8,128)(2,1)}, bf16[256,768]{1,0:T(8,128)(2,1)}, u32[]{:S(2)}, u32[]{:S(2)}) collective-permute-start(bf16[256,768]{1,0:T(8,128)(2,1)} %slice.22), channel_id=1, source_target_pairs={{0,2},{2,0},{1,3},{3,1},{4,6},{6,4},{5,7},{7,5},{8,10},{10,8},{9,1... | collective-permute-start | bytes 1179656 | tf_op jit(solution)/shard_map/ppermute | solution.py:278
  9.3 2.5 %copy-start.9 = (f32[128]{0:T(128)S(1)}, f32[128]{0:T(128)}, u32[]{:S(2)}) copy-start(f32[128]{0:T(128)} %param.14) | copy-start | bytes 1540
  9.8 2.0 %collective-permute-start.2 = (bf16[128,768]{1,0:T(8,128)(2,1)}, bf16[128,768]{1,0:T(8,128)(2,1)}, u32[]{:S(2)}, u32[]{:S(2)}) collective-permute-start(bf16[128,768]{1,0:T(8,128)(2,1)} %collective-permute-done.1.refs_2_), channel_id=1, source_target_pairs={{0,1},{1,0},{2,3},{3,2},{4,5},{5,4},{6,7},{7,6},{8,9},{9,8},{10,11... | collective-permute-start | bytes 589832 | tf_op jit(solution)/shard_map/ppermute | solution.py:278
  9.8 20.9 %collective-permute-start.8 = (bf16[384,768]{1,0:T(8,128)(2,1)}, bf16[384,768]{1,0:T(8,128)(2,1)}, u32[]{:S(2)}, u32[]{:S(2)}) collective-permute-start(bf16[384,768]{1,0:T(8,128)(2,1)} %slice.19), channel_id=1, source_target_pairs={{0,2},{2,0},{1,3},{3,1},{4,6},{6,4},{5,7},{7,5},{8,10},{10,8},{9,1... | collective-permute-start | bytes 1769480 | tf_op jit(solution)/shard_map/ppermute | solution.py:278
  12.7 10.9 %copy-start.3 = (f32[3,3072]{1,0:T(4,128)S(1)}, f32[3,3072]{1,0:T(4,128)}, u32[]{:S(2)}) copy-start(f32[3,3072]{1,0:T(4,128)} %refs_6_.1) | copy-start | bytes 110596
  18.2 5.3 %collective-permute-start.6 = (bf16[256,768]{1,0:T(8,128)(2,1)}, bf16[256,768]{1,0:T(8,128)(2,1)S(1)}, u32[]{:S(2)}, u32[]{:S(2)}) collective-permute-start(bf16[256,768]{1,0:T(8,128)(2,1)} %collective-permute-done.5.refs_2_), channel_id=1, source_target_pairs={{0,1},{1,0},{2,3},{3,2},{4,5},{5,4},{6,7},{7,6},{8,9},{9,8},{10,11... | collective-permute-start | bytes 1179656 | tf_op jit(solution)/shard_map/ppermute | solution.py:278
  18.2 12.5 %collective-permute-start.4 = (bf16[144,256]{1,0:T(8,128)(2,1)S(1)}, bf16[144,256]{1,0:T(8,128)(2,1)S(1)}, u32[]{:S(2)}, u32[]{:S(2)}) collective-permute-start(bf16[144,256]{1,0:T(8,128)(2,1)S(1)} %get-tuple-element.31.refs_2_.refs_4_), channel_id=1, source_target_pairs={{0,8},{4,12},{8,0},{12,4},{1,9},{5,13},{9,1},{13,5},{2,10},{6,14},... | collective-permute-start | bytes 221192 | tf_op jit(solution)/shard_map/ppermute | solution.py:354
  21.3 9.4 %collective-permute-start.3 = (bf16[144,256]{1,0:T(8,128)(2,1)S(1)}, bf16[144,256]{1,0:T(8,128)(2,1)S(1)}, u32[]{:S(2)}, u32[]{:S(2)}) collective-permute-start(bf16[144,256]{1,0:T(8,128)(2,1)S(1)} %get-tuple-element.31.refs_2_.refs_4_), channel_id=1, source_target_pairs={{0,4},{4,0},{8,12},{12,8},{1,5},{5,1},{9,13},{13,9},{2,6},{6,2},{1... | collective-permute-start | bytes 221192 | tf_op jit(solution)/shard_map/ppermute | solution.py:353
  23.5 3.3 %copy-start.5 = (bf16[256,256]{1,0:T(8,128)(2,1)S(1)}, bf16[256,256]{1,0:T(8,128)(2,1)}, u32[]{:S(2)}) copy-start(bf16[256,256]{1,0:T(8,128)(2,1)} %refs_12_.1) | copy-start | bytes 393220
  23.5 3.3 %copy-start.6 = (s32[8,27]{1,0:T(8,128)S(1)}, s32[8,27]{1,0:T(8,128)}, u32[]{:S(2)}) copy-start(s32[8,27]{1,0:T(8,128)} %windows_ref.7) | copy-start | bytes 2596
  30.7 5.0 %collective-permute-start.9 = (bf16[384,768]{1,0:T(8,128)(2,1)}, bf16[384,768]{1,0:T(8,128)(2,1)S(1)}, u32[]{:S(2)}, u32[]{:S(2)}) collective-permute-start(bf16[384,768]{1,0:T(8,128)(2,1)} %collective-permute-done.8.refs_2_), channel_id=1, source_target_pairs={{0,1},{1,0},{2,3},{3,2},{4,5},{5,4},{6,7},{7,6},{8,9},{9,8},{10,11... | collective-permute-start | bytes 1769480 | tf_op jit(solution)/shard_map/ppermute | solution.py:278
  30.7 13.1 %collective-permute-start.13 = (bf16[256,256]{1,0:T(8,128)(2,1)S(1)}, bf16[256,256]{1,0:T(8,128)(2,1)S(1)}, u32[]{:S(2)}, u32[]{:S(2)}) collective-permute-start(bf16[256,256]{1,0:T(8,128)(2,1)S(1)} %get-tuple-element.41.refs_3_.refs_5_), channel_id=1, source_target_pairs={{0,4},{4,0},{8,12},{12,8},{1,5},{5,1},{9,13},{13,9},{2,6},{6,2},{1... | collective-permute-start | bytes 393224 | tf_op jit(solution)/shard_map/ppermute | solution.py:353
  32.6 11.2 %collective-permute-start.7 = (bf16[144,256]{1,0:T(8,128)(2,1)S(1)}, bf16[144,256]{1,0:T(8,128)(2,1)S(1)}, u32[]{:S(2)}, u32[]{:S(2)}) collective-permute-start(bf16[144,256]{1,0:T(8,128)(2,1)S(1)} %collective-permute-done.4.refs_7_), channel_id=1, source_target_pairs={{0,4},{4,0},{8,12},{12,8},{1,5},{5,1},{9,13},{13,9},{2,6},{6,2},{1... | collective-permute-start | bytes 221192 | tf_op jit(solution)/shard_map/ppermute | solution.py:353
  32.8 8.5 %collective-permute-start.10 = (bf16[256,256]{1,0:T(8,128)(2,1)S(1)}, bf16[256,256]{1,0:T(8,128)(2,1)S(1)}, u32[]{:S(2)}, u32[]{:S(2)}) collective-permute-start(bf16[256,256]{1,0:T(8,128)(2,1)S(1)} %get-tuple-element.41.refs_3_.refs_5_), channel_id=1, source_target_pairs={{0,8},{4,12},{8,0},{12,4},{1,9},{5,13},{9,1},{13,5},{2,10},{6,14},... | collective-permute-start | bytes 393224 | tf_op jit(solution)/shard_map/ppermute | solution.py:354
  39.7 13.5 %collective-permute-start.12 = (bf16[384,256]{1,0:T(8,128)(2,1)S(1)}, bf16[384,256]{1,0:T(8,128)(2,1)S(1)}, u32[]{:S(2)}, u32[]{:S(2)}) collective-permute-start(bf16[384,256]{1,0:T(8,128)(2,1)S(1)} %get-tuple-element.42.refs_3_), channel_id=1, source_target_pairs={{0,4},{4,0},{8,12},{12,8},{1,5},{5,1},{9,13},{13,9},{2,6},{6,2},{1... | collective-permute-start | bytes 589832 | tf_op jit(solution)/shard_map/ppermute | solution.py:353
  41.3 11.9 %collective-permute-start.11 = (bf16[384,256]{1,0:T(8,128)(2,1)S(1)}, bf16[384,256]{1,0:T(8,128)(2,1)S(1)}, u32[]{:S(2)}, u32[]{:S(2)}) collective-permute-start(bf16[384,256]{1,0:T(8,128)(2,1)S(1)} %get-tuple-element.42.refs_3_), channel_id=1, source_target_pairs={{0,8},{4,12},{8,0},{12,4},{1,9},{5,13},{9,1},{13,5},{2,10},{6,14},... | collective-permute-start | bytes 589832 | tf_op jit(solution)/shard_map/ppermute | solution.py:354
  43.9 9.3 %collective-permute-start.14 = (bf16[256,256]{1,0:T(8,128)(2,1)S(1)}, bf16[256,256]{1,0:T(8,128)(2,1)S(1)}, u32[]{:S(2)}, u32[]{:S(2)}) collective-permute-start(bf16[256,256]{1,0:T(8,128)(2,1)S(1)} %collective-permute-done.10.refs_10_), channel_id=1, source_target_pairs={{0,4},{4,0},{8,12},{12,8},{1,5},{5,1},{9,13},{13,9},{2,6},{6,2},{1... | collective-permute-start | bytes 393224 | tf_op jit(solution)/shard_map/ppermute | solution.py:353
  53.2 5.7 %collective-permute-start.15 = (bf16[384,256]{1,0:T(8,128)(2,1)S(1)}, bf16[384,256]{1,0:T(8,128)(2,1)S(1)}, u32[]{:S(2)}, u32[]{:S(2)}) collective-permute-start(bf16[384,256]{1,0:T(8,128)(2,1)S(1)} %collective-permute-done.11.refs_5_), channel_id=1, source_target_pairs={{0,4},{4,0},{8,12},{12,8},{1,5},{5,1},{9,13},{13,9},{2,6},{6,2},{1... | collective-permute-start | bytes 589832 | tf_op jit(solution)/shard_map/ppermute | solution.py:353
  57.8 9.9 %copy-start.4 = (bf16[512,768]{1,0:T(8,128)(2,1)S(1)}, bf16[512,768]{1,0:T(8,128)(2,1)}, u32[]{:S(2)}) copy-start(bf16[512,768]{1,0:T(8,128)(2,1)} %refs_4_.8) | copy-start | bytes 2359300
  60.5 5.7 %collective-permute-start.17 = (bf16[768,128]{1,0:T(8,128)(2,1)S(1)}, bf16[768,128]{1,0:T(8,128)(2,1)S(1)}, u32[]{:S(2)}, u32[]{:S(2)}) collective-permute-start(bf16[768,128]{1,0:T(8,128)(2,1)S(1)} %shard_map.107.refs_0_), channel_id=1, source_target_pairs={{0,2},{2,0},{1,3},{3,1},{4,6},{6,4},{5,7},{7,5},{8,10},{10,8},{9,1... | collective-permute-start | bytes 589832 | tf_op jit(solution)/shard_map/ppermute | solution.py:278
  62.1 4.2 %collective-permute-start.16 = (bf16[768,128]{1,0:T(8,128)(2,1)S(1)}, bf16[768,128]{1,0:T(8,128)(2,1)S(1)}, u32[]{:S(2)}, u32[]{:S(2)}) collective-permute-start(bf16[768,128]{1,0:T(8,128)(2,1)S(1)} %shard_map.107.refs_0_), channel_id=1, source_target_pairs={{0,1},{1,0},{2,3},{3,2},{4,5},{5,4},{6,7},{7,6},{8,9},{9,8},{10,11... | collective-permute-start | bytes 589832 | tf_op jit(solution)/shard_map/ppermute | solution.py:278
  66.3 1.4 %collective-permute-start.18 = (bf16[768,128]{1,0:T(8,128)(2,1)S(1)}, bf16[768,128]{1,0:T(8,128)(2,1)S(1)}, u32[]{:S(2)}, u32[]{:S(2)}) collective-permute-start(bf16[768,128]{1,0:T(8,128)(2,1)S(1)} %collective-permute-done.17.refs_2_), channel_id=1, source_target_pairs={{0,1},{1,0},{2,3},{3,2},{4,5},{5,4},{6,7},{7,6},{8,9},{9,8},{10,11... | collective-permute-start | bytes 589832 | tf_op jit(solution)/shard_map/ppermute | solution.py:278
  (5 other events, 10.0 us)

commit v3 on v2

--- a/solution.py
+++ b/solution.py
@@ -140,6 +140,8 @@
     if last:
         out_ref = refs.pop(0)
     shift_ref, total_ref, accum_ref, query_ref = refs
+    kept = last and not begin
+    shifts_ref = shift_in if kept else shift_ref
     for start, piece in zip(starts, queries):
         query_ref[start : start + piece.shape[0], :] = piece[...]
     if begin:
@@ -160,7 +162,8 @@
                 weights.astype(jnp.bfloat16), text_ref[:, HD:], preferred_element_type=jnp.float32
             )
         else:
-            shift_ref[rows, :] = shift_in[rows, :]
+            if not kept:
+                shift_ref[rows, :] = shift_in[rows, :]
             total_ref[rows, :] = total_in[rows, :]
             accum_ref[rows, :] = accum_in[rows, :]
         own = own_ref[tile]
@@ -179,7 +182,7 @@
                 def _():
                     parts = [
                         attend_block(
-                            query_ref[rows, :], shift_ref[rows, :], view(number)[span, :HD], view(number)[span, HD:]
+                            query_ref[rows, :], shifts_ref[rows, :], view(number)[span, :HD], view(number)[span, HD:]
                         )
                         for number, span in blocks
                     ]

time: 70 us -> 69.6 us (level)
  Pallas kernels: 22.8 us -> 18.2 us
  waiting for transfers between devices: 14.6 us -> 18.4 us
    pallas_call x4, Pallas kernels: 10.7 us -> 6.13 us  [attend(): pl.pallas_call(functools.partial(attend_kernel, [at for at, array in quer...]
    ppermute x6, waiting for transfers between devices: 3.16 us -> 6.89 us  [body(): near = lambda values: lax.ppermute(values, 'tiles', NEAR)]
  transfers between devices with their start and end apart: 19 -> 19, of which waited for: 7 -> 7; matrix products, arithmetic and copies ran while one was open for 7% -> 7% of each run, Pallas kernels for 27% -> 22%
where the time goes in v3:
time: 69.6 us; the launch traced here: 69.2 us
  starting transfers between devices  24.4 us (35%)
  waiting for transfers between devices  18.4 us (26%)
  Pallas kernels  18.2 us (26%)
  local copies, waits for them, and re-layouts  7.12 us (10%)
  between operations  0.84 us (1%)
    ppermute x10, waiting for transfers between devices, shifted(): lax.ppermute(values, axis, [(at, (at + by) % size) for at in range(size)])  11.5 us
    pallas_call x3, Pallas kernels, project(): pl.pallas_call(functools.partial(project_kernel, count, len(after), start...  9.7 us
    ppermute x6, starting transfers between devices, body(): near = lambda values: lax.ppermute(values, 'tiles', NEAR)  9.46 us
    ppermute x3, starting transfers between devices, body(): away = lambda values: lax.ppermute(values, 'tiles', AWAY)  8.43 us
    ppermute x6, waiting for transfers between devices, body(): near = lambda values: lax.ppermute(values, 'tiles', NEAR)  6.89 us
    ppermute x10, starting transfers between devices, shifted(): lax.ppermute(values, axis, [(at, (at + by) % size) for at in range(size)])  6.53 us
    pallas_call x4, Pallas kernels, attend(): pl.pallas_call(functools.partial(attend_kernel, [at for at, array in quer...  6.13 us
    slice x2, local copies, waits for them, and re-layouts, body(): parts += [rest[start:start + size] for start, size in CHUNKS[1:]]  3.68 us
  transfers between devices with their start and end apart: 19, of which 7 were waited for; matrix products, arithmetic and copies ran while one was open for 7% of the time, Pallas kernels for 22%

profile of v3, /device:TPU:0, one launch (start us, length us, event | category | flops | bytes accessed | tf_op | source)
XLA Modules:
  0.0 69.2 jit_solution(8716807022995479661)
XLA Ops:
  1.4 2.6 %collective-permute-start.1 = (bf16[128,768]{1,0:T(8,128)(2,1)S(1)}, bf16[128,768]{1,0:T(8,128)(2,1)}, u32[]{:S(2)}, u32[]{:S(2)}) collective-permute-start(bf16[128,768]{1,0:T(8,128)(2,1)S(1)} %slice.18), channel_id=1, source_target_pairs={{0,2},{2,0},{1,3},{3,1},{4,6},{6,4},{5,7},{7,5},{8,10},{10,8},{9,1... | collective-permute-start | bytes 589832 | tf_op jit(solution)/shard_map/ppermute | solution.py:281
  4.0 1.8 %slice.22 = bf16[256,768]{1,0:T(8,128)(2,1)} slice(bf16[768,768]{1,0:T(8,128)(2,1)} %refs_5_.3), slice={[128:384], [0:768]} | slice | bytes 786432 | tf_op jit(solution)/shard_map/slice | solution.py:324
  5.7 1.9 %slice.19 = bf16[384,768]{1,0:T(8,128)(2,1)} slice(bf16[768,768]{1,0:T(8,128)(2,1)} %refs_5_.3), slice={[384:768], [0:768]} | slice | bytes 1179648 | tf_op jit(solution)/shard_map/slice | solution.py:324
  7.7 1.7 %copy-done.1 = bf16[3072,384]{1,0:T(8,128)(2,1)S(1)} copy-done((bf16[3072,384]{1,0:T(8,128)(2,1)S(1)}, bf16[3072,384]{1,0:T(8,128)(2,1)}, u32[]{:S(2)}) %copy-start.1) | copy-done | bytes 2359320
  9.8 1.9 %collective-permute-start.8 = (bf16[384,768]{1,0:T(8,128)(2,1)}, bf16[384,768]{1,0:T(8,128)(2,1)}, u32[]{:S(2)}, u32[]{:S(2)}) collective-permute-start(bf16[384,768]{1,0:T(8,128)(2,1)} %slice.19), channel_id=1, source_target_pairs={{0,2},{2,0},{1,3},{3,1},{4,6},{6,4},{5,7},{7,5},{8,10},{10,8},{9,1... | collective-permute-start | bytes 1769480 | tf_op jit(solution)/shard_map/ppermute | solution.py:281
  12.7 2.5 %shard_map.101 = (bf16[128,128]{1,0:T(8,128)(2,1)S(1)}, bf16[144,256]{1,0:T(8,128)(2,1)S(1)}) custom-call(s32[4]{0:T(128)S(1)} %pad_add_fusion.place_ref, s32[2]{0:T(128)S(1)} %copy-done.7, bf16[768,768]{1,0:T(8,128)(2,1)S(1)} %copy-done, bf16[768,768]{1,0:T(8,128)(2,1)} %collective-permute-done.refs_1_, bf16[128,768]{1,0:T(8,128)(2,1)} %collective-permute-done.1.refs_2_, ...), custom_call_target="tpu_custom_call" | custom-call | flops 128 | bytes 128 | tf_op jit(solution)/shard_map/pallas_call | solution.py:99
  15.2 3.1 %collective-permute-done.5.refs_2_ = bf16[256,768]{1,0:T(8,128)(2,1)} collective-permute-done((bf16[256,768]{1,0:T(8,128)(2,1)}, bf16[256,768]{1,0:T(8,128)(2,1)}, u32[]{:S(2)}, u32[]{:S(2)}) %collective-permute-start.5) | collective-permute-done | bytes 393248 | tf_op jit(solution)/shard_map/ppermute | solution.py:281
  18.2 3.0 %collective-permute-start.4 = (bf16[144,256]{1,0:T(8,128)(2,1)S(1)}, bf16[144,256]{1,0:T(8,128)(2,1)S(1)}, u32[]{:S(2)}, u32[]{:S(2)}) collective-permute-start(bf16[144,256]{1,0:T(8,128)(2,1)S(1)} %get-tuple-element.31.refs_2_.refs_4_), channel_id=1, source_target_pairs={{0,8},{4,12},{8,0},{12,4},{1,9},{5,13},{9,1},{13,5},{2,10},{6,14},... | collective-permute-start | bytes 221192 | tf_op jit(solution)/shard_map/ppermute | solution.py:357
  21.3 1.6 %collective-permute-start.3 = (bf16[144,256]{1,0:T(8,128)(2,1)S(1)}, bf16[144,256]{1,0:T(8,128)(2,1)S(1)}, u32[]{:S(2)}, u32[]{:S(2)}) collective-permute-start(bf16[144,256]{1,0:T(8,128)(2,1)S(1)} %get-tuple-element.31.refs_2_.refs_4_), channel_id=1, source_target_pairs={{0,4},{4,0},{8,12},{12,8},{1,5},{5,1},{9,13},{13,9},{2,6},{6,2},{1... | collective-permute-start | bytes 221192 | tf_op jit(solution)/shard_map/ppermute | solution.py:356
  23.6 3.2 %shard_map.102 = (bf16[256,128]{1,0:T(8,128)(2,1)S(1)}, bf16[256,256]{1,0:T(8,128)(2,1)S(1)}) custom-call(s32[4]{0:T(128)S(1)} %pad_add_fusion.place_ref, s32[2]{0:T(128)S(1)} %copy-done.7, bf16[768,768]{1,0:T(8,128)(2,1)S(1)} %copy-done, bf16[768,768]{1,0:T(8,128)(2,1)} %collective-permute-done.refs_1_, bf16[256,768]{1,0:T(8,128)(2,1)} %collective-permute-done.5.refs_2_, ...), custom_call_target="tpu_custom_call" | custom-call | flops 256 | bytes 256 | tf_op jit(solution)/shard_map/pallas_call | solution.py:99
  28.2 2.5 %collective-permute-done.8.refs_2_ = bf16[384,768]{1,0:T(8,128)(2,1)} collective-permute-done((bf16[384,768]{1,0:T(8,128)(2,1)}, bf16[384,768]{1,0:T(8,128)(2,1)}, u32[]{:S(2)}, u32[]{:S(2)}) %collective-permute-start.8) | collective-permute-done | bytes 589856 | tf_op jit(solution)/shard_map/ppermute | solution.py:281
  30.7 1.9 %collective-permute-start.13 = (bf16[256,256]{1,0:T(8,128)(2,1)S(1)}, bf16[256,256]{1,0:T(8,128)(2,1)S(1)}, u32[]{:S(2)}, u32[]{:S(2)}) collective-permute-start(bf16[256,256]{1,0:T(8,128)(2,1)S(1)} %get-tuple-element.41.refs_3_.refs_5_), channel_id=1, source_target_pairs={{0,4},{4,0},{8,12},{12,8},{1,5},{5,1},{9,13},{13,9},{2,6},{6,2},{1... | collective-permute-start | bytes 393224 | tf_op jit(solution)/shard_map/ppermute | solution.py:356
  32.8 2.8 %collective-permute-start.10 = (bf16[256,256]{1,0:T(8,128)(2,1)S(1)}, bf16[256,256]{1,0:T(8,128)(2,1)S(1)}, u32[]{:S(2)}, u32[]{:S(2)}) collective-permute-start(bf16[256,256]{1,0:T(8,128)(2,1)S(1)} %get-tuple-element.41.refs_3_.refs_5_), channel_id=1, source_target_pairs={{0,8},{4,12},{8,0},{12,4},{1,9},{5,13},{9,1},{13,5},{2,10},{6,14},... | collective-permute-start | bytes 393224 | tf_op jit(solution)/shard_map/ppermute | solution.py:357
  35.7 4.0 %shard_map.104 = (bf16[384,128]{1,0:T(8,128)(2,1)S(1)}, bf16[384,256]{1,0:T(8,128)(2,1)S(1)}) custom-call(s32[4]{0:T(128)S(1)} %pad_add_fusion.place_ref, s32[2]{0:T(128)S(1)} %copy-done.7, bf16[768,768]{1,0:T(8,128)(2,1)S(1)} %copy-done, bf16[768,768]{1,0:T(8,128)(2,1)} %collective-permute-done.refs_1_, bf16[384,768]{1,0:T(8,128)(2,1)} %collective-permute-done.8.refs_2_, ...), custom_call_target="tpu_custom_call" | custom-call | flops 384 | bytes 384 | tf_op jit(solution)/shard_map/pallas_call | solution.py:99
  39.7 1.6 %collective-permute-start.12 = (bf16[384,256]{1,0:T(8,128)(2,1)S(1)}, bf16[384,256]{1,0:T(8,128)(2,1)S(1)}, u32[]{:S(2)}, u32[]{:S(2)}) collective-permute-start(bf16[384,256]{1,0:T(8,128)(2,1)S(1)} %get-tuple-element.42.refs_3_), channel_id=1, source_target_pairs={{0,4},{4,0},{8,12},{12,8},{1,5},{5,1},{9,13},{13,9},{2,6},{6,2},{1... | collective-permute-start | bytes 589832 | tf_op jit(solution)/shard_map/ppermute | solution.py:356
  41.3 2.6 %collective-permute-start.11 = (bf16[384,256]{1,0:T(8,128)(2,1)S(1)}, bf16[384,256]{1,0:T(8,128)(2,1)S(1)}, u32[]{:S(2)}, u32[]{:S(2)}) collective-permute-start(bf16[384,256]{1,0:T(8,128)(2,1)S(1)} %get-tuple-element.42.refs_3_), channel_id=1, source_target_pairs={{0,8},{4,12},{8,0},{12,4},{1,9},{5,13},{9,1},{13,5},{2,10},{6,14},... | collective-permute-start | bytes 589832 | tf_op jit(solution)/shard_map/ppermute | solution.py:357
  43.9 2.5 %collective-permute-start.14 = (bf16[256,256]{1,0:T(8,128)(2,1)S(1)}, bf16[256,256]{1,0:T(8,128)(2,1)S(1)}, u32[]{:S(2)}, u32[]{:S(2)}) collective-permute-start(bf16[256,256]{1,0:T(8,128)(2,1)S(1)} %collective-permute-done.10.refs_10_), channel_id=1, source_target_pairs={{0,4},{4,0},{8,12},{12,8},{1,5},{5,1},{9,13},{13,9},{2,6},{6,2},{1... | collective-permute-start | bytes 393224 | tf_op jit(solution)/shard_map/ppermute | solution.py:356
  46.5 2.7 %shard_map.105 = (f32[768,128]{1,0:T(8,128)S(1)}, f32[768,128]{1,0:T(8,128)S(1)}, f32[768,128]{1,0:T(8,128)S(1)}) custom-call(s32[8]{0:T(128)S(1)} %pad_add_fusion.1.ids_ref, s32[2]{0:T(128)S(1)} %copy-done.7, s32[8,27]{1,0:T(8,128)S(1)} %copy-done.6, bf16[128,128]{1,0:T(8,128)(2,1)S(1)} %get-tuple-element.35.refs_0_, ...), custom_call_target="tpu_custom_call" | custom-call | flops 1327104 | bytes 98304 | tf_op jit(solution)/shard_map/pallas_call | solution.py:219
  49.2 4.0 %collective-permute-done.14.refs_3_ = bf16[256,256]{1,0:T(8,128)(2,1)S(1)} collective-permute-done((bf16[256,256]{1,0:T(8,128)(2,1)S(1)}, bf16[256,256]{1,0:T(8,128)(2,1)S(1)}, u32[]{:S(2)}, u32[]{:S(2)}) %collective-permute-start.14) | collective-permute-done | bytes 131104 | tf_op jit(solution)/shard_map/ppermute | solution.py:356
  53.2 1.6 %collective-permute-start.15 = (bf16[384,256]{1,0:T(8,128)(2,1)S(1)}, bf16[384,256]{1,0:T(8,128)(2,1)S(1)}, u32[]{:S(2)}, u32[]{:S(2)}) collective-permute-start(bf16[384,256]{1,0:T(8,128)(2,1)S(1)} %collective-permute-done.11.refs_5_), channel_id=1, source_target_pairs={{0,4},{4,0},{8,12},{12,8},{1,5},{5,1},{9,13},{13,9},{2,6},{6,2},{1... | collective-permute-start | bytes 589832 | tf_op jit(solution)/shard_map/ppermute | solution.py:356
  55.9 2.9 %collective-permute-done.15.refs_3_ = bf16[384,256]{1,0:T(8,128)(2,1)S(1)} collective-permute-done((bf16[384,256]{1,0:T(8,128)(2,1)S(1)}, bf16[384,256]{1,0:T(8,128)(2,1)S(1)}, u32[]{:S(2)}, u32[]{:S(2)}) %collective-permute-start.15) | collective-permute-done | bytes 196640 | tf_op jit(solution)/shard_map/ppermute | solution.py:356
  59.8 1.6 %collective-permute-start.17 = (bf16[768,128]{1,0:T(8,128)(2,1)S(1)}, bf16[768,128]{1,0:T(8,128)(2,1)S(1)}, u32[]{:S(2)}, u32[]{:S(2)}) collective-permute-start(bf16[768,128]{1,0:T(8,128)(2,1)S(1)} %shard_map.107.refs_0_), channel_id=1, source_target_pairs={{0,2},{2,0},{1,3},{3,1},{4,6},{6,4},{5,7},{7,5},{8,10},{10,8},{9,1... | collective-permute-start | bytes 589832 | tf_op jit(solution)/shard_map/ppermute | solution.py:281
  61.3 4.2 %collective-permute-done.17.refs_2_ = bf16[768,128]{1,0:T(8,128)(2,1)S(1)} collective-permute-done((bf16[768,128]{1,0:T(8,128)(2,1)S(1)}, bf16[768,128]{1,0:T(8,128)(2,1)S(1)}, u32[]{:S(2)}, u32[]{:S(2)}) %collective-permute-start.17) | collective-permute-done | bytes 196640 | tf_op jit(solution)/shard_map/ppermute | solution.py:281
  66.9 2.2 %shard_map.108 = bf16[768,768]{1,0:T(8,128)(2,1)} custom-call(s32[4]{0:T(128)S(1)} %pad_add_fusion.place_ref, bf16[768,128]{1,0:T(8,128)(2,1)S(1)} %shard_map.107.refs_0_, bf16[768,128]{1,0:T(8,128)(2,1)S(1)} %collective-permute-done.16.refs_1_, bf16[768,128]{1,0:T(8,128)(2,1)S(1)} %collective-permute-done.17.refs_2_, ...), custom_call_target="tpu_custom_call" | custom-call | flops 603979776 | bytes 3932160 | tf_op jit(solution)/shard_map/pallas_call | solution.py:261
  (51 shorter events, 8.0 us)
Async XLA Ops:
  0.0 11.8 %collective-permute-start = (bf16[768,768]{1,0:T(8,128)(2,1)}, bf16[768,768]{1,0:T(8,128)(2,1)}, u32[]{:S(2)}, u32[]{:S(2)}) collective-permute-start(bf16[768,768]{1,0:T(8,128)(2,1)} %refs_5_.3), channel_id=1, source_target_pairs={{0,1},{1,0},{2,3},{3,2},{4,5},{5,4},{6,7},{7,6},{8,9},{9,8},{10,11... | collective-permute-start | bytes 3538952 | tf_op jit(solution)/shard_map/ppermute | solution.py:281
  1.4 8.4 %collective-permute-start.1 = (bf16[128,768]{1,0:T(8,128)(2,1)S(1)}, bf16[128,768]{1,0:T(8,128)(2,1)}, u32[]{:S(2)}, u32[]{:S(2)}) collective-permute-start(bf16[128,768]{1,0:T(8,128)(2,1)S(1)} %slice.18), channel_id=1, source_target_pairs={{0,2},{2,0},{1,3},{3,1},{4,6},{6,4},{5,7},{7,5},{8,10},{10,8},{9,1... | collective-permute-start | bytes 589832 | tf_op jit(solution)/shard_map/ppermute | solution.py:281
  5.7 12.5 %collective-permute-start.5 = (bf16[256,768]{1,0:T(8,128)(2,1)}, bf16[256,768]{1,0:T(8,128)(2,1)}, u32[]{:S(2)}, u32[]{:S(2)}) collective-permute-start(bf16[256,768]{1,0:T(8,128)(2,1)} %slice.22), channel_id=1, source_target_pairs={{0,2},{2,0},{1,3},{3,1},{4,6},{6,4},{5,7},{7,5},{8,10},{10,8},{9,1... | collective-permute-start | bytes 1179656 | tf_op jit(solution)/shard_map/ppermute | solution.py:281
  9.3 2.5 %copy-start.9 = (f32[128]{0:T(128)S(1)}, f32[128]{0:T(128)}, u32[]{:S(2)}) copy-start(f32[128]{0:T(128)} %param.14) | copy-start | bytes 1540
  9.8 2.0 %collective-permute-start.2 = (bf16[128,768]{1,0:T(8,128)(2,1)}, bf16[128,768]{1,0:T(8,128)(2,1)}, u32[]{:S(2)}, u32[]{:S(2)}) collective-permute-start(bf16[128,768]{1,0:T(8,128)(2,1)} %collective-permute-done.1.refs_2_), channel_id=1, source_target_pairs={{0,1},{1,0},{2,3},{3,2},{4,5},{5,4},{6,7},{7,6},{8,9},{9,8},{10,11... | collective-permute-start | bytes 589832 | tf_op jit(solution)/shard_map/ppermute | solution.py:281
  9.8 20.9 %collective-permute-start.8 = (bf16[384,768]{1,0:T(8,128)(2,1)}, bf16[384,768]{1,0:T(8,128)(2,1)}, u32[]{:S(2)}, u32[]{:S(2)}) collective-permute-start(bf16[384,768]{1,0:T(8,128)(2,1)} %slice.19), channel_id=1, source_target_pairs={{0,2},{2,0},{1,3},{3,1},{4,6},{6,4},{5,7},{7,5},{8,10},{10,8},{9,1... | collective-permute-start | bytes 1769480 | tf_op jit(solution)/shard_map/ppermute | solution.py:281
  12.7 10.9 %copy-start.3 = (f32[3,3072]{1,0:T(4,128)S(1)}, f32[3,3072]{1,0:T(4,128)}, u32[]{:S(2)}) copy-start(f32[3,3072]{1,0:T(4,128)} %refs_6_.1) | copy-start | bytes 110596
  18.2 5.3 %collective-permute-start.6 = (bf16[256,768]{1,0:T(8,128)(2,1)}, bf16[256,768]{1,0:T(8,128)(2,1)S(1)}, u32[]{:S(2)}, u32[]{:S(2)}) collective-permute-start(bf16[256,768]{1,0:T(8,128)(2,1)} %collective-permute-done.5.refs_2_), channel_id=1, source_target_pairs={{0,1},{1,0},{2,3},{3,2},{4,5},{5,4},{6,7},{7,6},{8,9},{9,8},{10,11... | collective-permute-start | bytes 1179656 | tf_op jit(solution)/shard_map/ppermute | solution.py:281
  18.2 12.5 %collective-permute-start.4 = (bf16[144,256]{1,0:T(8,128)(2,1)S(1)}, bf16[144,256]{1,0:T(8,128)(2,1)S(1)}, u32[]{:S(2)}, u32[]{:S(2)}) collective-permute-start(bf16[144,256]{1,0:T(8,128)(2,1)S(1)} %get-tuple-element.31.refs_2_.refs_4_), channel_id=1, source_target_pairs={{0,8},{4,12},{8,0},{12,4},{1,9},{5,13},{9,1},{13,5},{2,10},{6,14},... | collective-permute-start | bytes 221192 | tf_op jit(solution)/shard_map/ppermute | solution.py:357
  21.3 9.4 %collective-permute-start.3 = (bf16[144,256]{1,0:T(8,128)(2,1)S(1)}, bf16[144,256]{1,0:T(8,128)(2,1)S(1)}, u32[]{:S(2)}, u32[]{:S(2)}) collective-permute-start(bf16[144,256]{1,0:T(8,128)(2,1)S(1)} %get-tuple-element.31.refs_2_.refs_4_), channel_id=1, source_target_pairs={{0,4},{4,0},{8,12},{12,8},{1,5},{5,1},{9,13},{13,9},{2,6},{6,2},{1... | collective-permute-start | bytes 221192 | tf_op jit(solution)/shard_map/ppermute | solution.py:356
  23.5 3.3 %copy-start.5 = (bf16[256,256]{1,0:T(8,128)(2,1)S(1)}, bf16[256,256]{1,0:T(8,128)(2,1)}, u32[]{:S(2)}) copy-start(bf16[256,256]{1,0:T(8,128)(2,1)} %refs_12_.1) | copy-start | bytes 393220
  23.5 3.3 %copy-start.6 = (s32[8,27]{1,0:T(8,128)S(1)}, s32[8,27]{1,0:T(8,128)}, u32[]{:S(2)}) copy-start(s32[8,27]{1,0:T(8,128)} %windows_ref.7) | copy-start | bytes 2596
  30.7 5.0 %collective-permute-start.9 = (bf16[384,768]{1,0:T(8,128)(2,1)}, bf16[384,768]{1,0:T(8,128)(2,1)S(1)}, u32[]{:S(2)}, u32[]{:S(2)}) collective-permute-start(bf16[384,768]{1,0:T(8,128)(2,1)} %collective-permute-done.8.refs_2_), channel_id=1, source_target_pairs={{0,1},{1,0},{2,3},{3,2},{4,5},{5,4},{6,7},{7,6},{8,9},{9,8},{10,11... | collective-permute-start | bytes 1769480 | tf_op jit(solution)/shard_map/ppermute | solution.py:281
  30.7 13.1 %collective-permute-start.13 = (bf16[256,256]{1,0:T(8,128)(2,1)S(1)}, bf16[256,256]{1,0:T(8,128)(2,1)S(1)}, u32[]{:S(2)}, u32[]{:S(2)}) collective-permute-start(bf16[256,256]{1,0:T(8,128)(2,1)S(1)} %get-tuple-element.41.refs_3_.refs_5_), channel_id=1, source_target_pairs={{0,4},{4,0},{8,12},{12,8},{1,5},{5,1},{9,13},{13,9},{2,6},{6,2},{1... | collective-permute-start | bytes 393224 | tf_op jit(solution)/shard_map/ppermute | solution.py:356
  32.6 11.2 %collective-permute-start.7 = (bf16[144,256]{1,0:T(8,128)(2,1)S(1)}, bf16[144,256]{1,0:T(8,128)(2,1)S(1)}, u32[]{:S(2)}, u32[]{:S(2)}) collective-permute-start(bf16[144,256]{1,0:T(8,128)(2,1)S(1)} %collective-permute-done.4.refs_7_), channel_id=1, source_target_pairs={{0,4},{4,0},{8,12},{12,8},{1,5},{5,1},{9,13},{13,9},{2,6},{6,2},{1... | collective-permute-start | bytes 221192 | tf_op jit(solution)/shard_map/ppermute | solution.py:356
  32.8 8.5 %collective-permute-start.10 = (bf16[256,256]{1,0:T(8,128)(2,1)S(1)}, bf16[256,256]{1,0:T(8,128)(2,1)S(1)}, u32[]{:S(2)}, u32[]{:S(2)}) collective-permute-start(bf16[256,256]{1,0:T(8,128)(2,1)S(1)} %get-tuple-element.41.refs_3_.refs_5_), channel_id=1, source_target_pairs={{0,8},{4,12},{8,0},{12,4},{1,9},{5,13},{9,1},{13,5},{2,10},{6,14},... | collective-permute-start | bytes 393224 | tf_op jit(solution)/shard_map/ppermute | solution.py:357
  39.7 13.5 %collective-permute-start.12 = (bf16[384,256]{1,0:T(8,128)(2,1)S(1)}, bf16[384,256]{1,0:T(8,128)(2,1)S(1)}, u32[]{:S(2)}, u32[]{:S(2)}) collective-permute-start(bf16[384,256]{1,0:T(8,128)(2,1)S(1)} %get-tuple-element.42.refs_3_), channel_id=1, source_target_pairs={{0,4},{4,0},{8,12},{12,8},{1,5},{5,1},{9,13},{13,9},{2,6},{6,2},{1... | collective-permute-start | bytes 589832 | tf_op jit(solution)/shard_map/ppermute | solution.py:356
  41.3 11.9 %collective-permute-start.11 = (bf16[384,256]{1,0:T(8,128)(2,1)S(1)}, bf16[384,256]{1,0:T(8,128)(2,1)S(1)}, u32[]{:S(2)}, u32[]{:S(2)}) collective-permute-start(bf16[384,256]{1,0:T(8,128)(2,1)S(1)} %get-tuple-element.42.refs_3_), channel_id=1, source_target_pairs={{0,8},{4,12},{8,0},{12,4},{1,9},{5,13},{9,1},{13,5},{2,10},{6,14},... | collective-permute-start | bytes 589832 | tf_op jit(solution)/shard_map/ppermute | solution.py:357
  43.9 9.3 %collective-permute-start.14 = (bf16[256,256]{1,0:T(8,128)(2,1)S(1)}, bf16[256,256]{1,0:T(8,128)(2,1)S(1)}, u32[]{:S(2)}, u32[]{:S(2)}) collective-permute-start(bf16[256,256]{1,0:T(8,128)(2,1)S(1)} %collective-permute-done.10.refs_10_), channel_id=1, source_target_pairs={{0,4},{4,0},{8,12},{12,8},{1,5},{5,1},{9,13},{13,9},{2,6},{6,2},{1... | collective-permute-start | bytes 393224 | tf_op jit(solution)/shard_map/ppermute | solution.py:356
  53.2 5.7 %collective-permute-start.15 = (bf16[384,256]{1,0:T(8,128)(2,1)S(1)}, bf16[384,256]{1,0:T(8,128)(2,1)S(1)}, u32[]{:S(2)}, u32[]{:S(2)}) collective-permute-start(bf16[384,256]{1,0:T(8,128)(2,1)S(1)} %collective-permute-done.11.refs_5_), channel_id=1, source_target_pairs={{0,4},{4,0},{8,12},{12,8},{1,5},{5,1},{9,13},{13,9},{2,6},{6,2},{1... | collective-permute-start | bytes 589832 | tf_op jit(solution)/shard_map/ppermute | solution.py:356
  55.9 11.0 %copy-start.4 = (bf16[512,768]{1,0:T(8,128)(2,1)S(1)}, bf16[512,768]{1,0:T(8,128)(2,1)}, u32[]{:S(2)}) copy-start(bf16[512,768]{1,0:T(8,128)(2,1)} %refs_4_.8) | copy-start | bytes 2359300
  59.8 5.7 %collective-permute-start.17 = (bf16[768,128]{1,0:T(8,128)(2,1)S(1)}, bf16[768,128]{1,0:T(8,128)(2,1)S(1)}, u32[]{:S(2)}, u32[]{:S(2)}) collective-permute-start(bf16[768,128]{1,0:T(8,128)(2,1)S(1)} %shard_map.107.refs_0_), channel_id=1, source_target_pairs={{0,2},{2,0},{1,3},{3,1},{4,6},{6,4},{5,7},{7,5},{8,10},{10,8},{9,1... | collective-permute-start | bytes 589832 | tf_op jit(solution)/shard_map/ppermute | solution.py:281
  61.3 4.2 %collective-permute-start.16 = (bf16[768,128]{1,0:T(8,128)(2,1)S(1)}, bf16[768,128]{1,0:T(8,128)(2,1)S(1)}, u32[]{:S(2)}, u32[]{:S(2)}) collective-permute-start(bf16[768,128]{1,0:T(8,128)(2,1)S(1)} %shard_map.107.refs_0_), channel_id=1, source_target_pairs={{0,1},{1,0},{2,3},{3,2},{4,5},{5,4},{6,7},{7,6},{8,9},{9,8},{10,11... | collective-permute-start | bytes 589832 | tf_op jit(solution)/shard_map/ppermute | solution.py:281
  65.5 1.4 %collective-permute-start.18 = (bf16[768,128]{1,0:T(8,128)(2,1)S(1)}, bf16[768,128]{1,0:T(8,128)(2,1)S(1)}, u32[]{:S(2)}, u32[]{:S(2)}) collective-permute-start(bf16[768,128]{1,0:T(8,128)(2,1)S(1)} %collective-permute-done.17.refs_2_), channel_id=1, source_target_pairs={{0,1},{1,0},{2,3},{3,2},{4,5},{5,4},{6,7},{7,6},{8,9},{9,8},{10,11... | collective-permute-start | bytes 589832 | tf_op jit(solution)/shard_map/ppermute | solution.py:281
  (5 other events, 10.0 us)
